TPU v7x, 512 devices: a whole 4x4x16 slice. The times are simulated.
512 devices in a mesh: dp: 256 (over x, z, y_hi, core), feat: 2 (over y_lo).
Axes of the slice: x: 4, y: 4 (y_hi: 2, y_lo: 2; y = y_hi * 2 + y_lo), z: 16, core: 2. Of those that a mesh axis runs over, the one named last changes fastest.
Arguments:
- image_feats: bfloat16 [32768, 1536], P('dp'), may hold values from -6 to 6
- text_emb: bfloat16 [32768, 1536], P('dp', 'feat'), may hold values from -6 to 6
- image_proj: bfloat16 [1536, 1536], P(None, 'feat'), may hold values from -0.15625 to 0.15625
- log_temp: float32 [1], replicated, may hold values from 4.1 to 4.8
- bias: float32 [1], replicated, may hold values from -4 to -1
Outputs:
- image_grad: float32 [32768, 1536], P('dp', 'feat')
- text_grad: float32 [32768, 1536], P('dp', 'feat')
All inputs are finite; a program needn't handle non-finite values.
Results may differ from a plain program's by a relative error of at most 0.0059.
Values may be sent and summed in bfloat16 or wider, within the bound.
A program may use at most 64 MiB of HBM per device.

v0:
```python
import jax
import jax.numpy as jnp
from jax import lax
from jax.sharding import PartitionSpec as P

EPS = 1e-06


def as_sent(x):
    return jax.tree.map(lambda a: a.astype(jnp.bfloat16) if a.dtype == jnp.float32 else a, x)


def from_partner(value, axis, distance):
    mask = 2**distance
    pairs = [(source, source ^ mask) for source in range(lax.axis_size(axis))]
    return lax.ppermute(value, axis, pairs)


def inner_rows(left, right):
    return lax.dot_general(
        left, right, (((1,), (1,)), ((), ())), preferred_element_type=jnp.float32
    )


def inner_cols(left, right):
    return lax.dot_general(
        left, right, (((0,), (0,)), ((), ())), preferred_element_type=jnp.float32
    )


def swap_first(blocks):
    return from_partner((as_sent(blocks[0]), as_sent(blocks[1])), "dp", 0)


def swap_second(blocks):
    return from_partner((as_sent(blocks[0]), as_sent(blocks[1])), "dp", 1)


def swap_third(blocks):
    return from_partner((as_sent(blocks[0]), as_sent(blocks[1])), "dp", 2)


def swap_fourth(blocks):
    return from_partner((as_sent(blocks[0]), as_sent(blocks[1])), "dp", 3)


def local(image_feats, text_emb, image_proj, log_temp, bias):
    rows = image_feats.shape[0]
    group = 16
    img_emb = jnp.dot(image_feats, image_proj, preferred_element_type=jnp.float32)
    txt_emb = text_emb.astype(jnp.float32)
    img_sq, txt_sq = lax.psum(
        (jnp.sum(img_emb * img_emb, axis=1), jnp.sum(txt_emb * txt_emb, axis=1)), "feat"
    )
    img_norm = jnp.sqrt(img_sq + EPS)[:, None]
    txt_norm = jnp.sqrt(txt_sq + EPS)[:, None]
    img_unit32 = img_emb / img_norm
    txt_unit32 = txt_emb / txt_norm
    img_unit = img_unit32.astype(jnp.bfloat16)
    txt_unit = txt_unit32.astype(jnp.bfloat16)
    scale = jnp.exp(log_temp[0])
    offset = bias[0]

    def weigh(partial_value, diagonal):
        return (jax.nn.sigmoid(scale * partial_value + offset) - diagonal).astype(jnp.bfloat16)

    def partner_blocks(step, blocks):
        which = (
            (step % 2 == 0).astype(jnp.int32)
            + (step % 4 == 0).astype(jnp.int32)
            + (step % 8 == 0).astype(jnp.int32)
        )
        return lax.switch(which, [swap_first, swap_second, swap_third, swap_fourth], blocks)

    diagonal = jnp.eye(rows, dtype=jnp.float32)

    def add_split(acc, blocks, diag):
        img_block, txt_block = blocks
        first_sum, second_sum = lax.psum(
            (inner_rows(img_unit, txt_block), inner_rows(img_block, txt_unit)), "feat"
        )
        first = weigh(first_sum, diag)
        second = weigh(second_sum, diag.T)
        return (
            acc[0] + scale * jnp.dot(first, txt_block, preferred_element_type=jnp.float32),
            acc[1] + scale * inner_cols(second, img_block),
        )

    empty = jnp.zeros(img_emb.shape, jnp.float32)
    blocks = (img_unit, txt_unit)
    totals = (empty, empty)
    totals = add_split(totals, blocks, diagonal)
    blank = jnp.zeros_like(diagonal)

    def step_once(step, carry):
        moved, acc = carry
        moved = partner_blocks(step, moved)
        return (moved, add_split(acc, moved, blank))

    moved, totals = lax.fori_loop(1, group, step_once, (blocks, totals))
    img_back, txt_back = totals
    img_dot, txt_dot = lax.psum(
        (jnp.sum(img_unit32 * img_back, axis=1), jnp.sum(txt_unit32 * txt_back, axis=1)), "feat"
    )
    img_dir = ((img_back - img_unit32 * img_dot[:, None]) / img_norm).astype(jnp.bfloat16)
    text_grad = (txt_back - txt_unit32 * txt_dot[:, None]) / txt_norm
    img_part = inner_rows(img_dir, image_proj)
    image_grad = lax.psum_scatter(img_part, "feat", scatter_dimension=1, tiled=True)
    return (image_grad, text_grad)


def solution(mesh):
    placed = (P("dp", None), P("dp", "feat"), P(None, "feat"), P(), P())
    return jax.shard_map(
        local,
        mesh=mesh,
        in_specs=placed,
        out_specs=(P("dp", "feat"), P("dp", "feat")),
        check_vma=False,
    )
```

profile of v0, /device:TPU:1, one launch (start us, length us, event | category | flops | bytes accessed | tf_op | source)
XLA Modules:
  0.0 1045.9 jit_solution(12005447582939628842)
XLA Ops:
  18.7 45.7 %all-reduce.8.cloned.1.call-done = f32[128,128]{1,0:T(8,128)} async-done(((f32[128,128]{1,0:T(8,128)}), f32[128,128]{1,0:T(8,128)}) %all-reduce.8.cloned.1.call-update) | async-done | bytes 65552 | tf_op jit(solution)/shard_map/psum | solution.py:79
  66.5 933.3 %while.22 = (s32[]{:T(128)}, bf16[128,768]{1,0:T(8,128)(2,1)}, bf16[128,768]{1,0:T(8,128)(2,1)}, f32[128,768]{1,0:T(8,128)S(1)}, f32[128,768]{1,0:T(8,128)S(1)},...) while((s32[]{:T(128)}, bf16[128,768]{1,0:T(8,128)(2,1)}, ...), condition=%wide.region_12.13_spmd, body=%wide.region_5.12_spmd.sunk | while | flops 101285920 | bytes 6161050 | solution.py:100
  80.1 40.7 %all-reduce.10.cloned.1.call-done = (f32[128,128]{1,0:T(8,128)}, f32[128,128]{1,0:T(8,128)}) async-done(((f32[128,128]{1,0:T(8,128)}, f32[128,128]{1,0:T(8,128)}), (f32[128,128]{1,0:T(8,128)}, f32[128,128]{1,0:T(8,128)})) %all-reduce.10.cloned.1.call-update) | async-done | bytes 131088 | tf_op jit(solution)/shard_map/while/body/eval_jaxpr/psum | solution.py:79
  124.6 13.1 %conditional.2 = (bf16[128,768]{1,0:T(8,128)(2,1)}, bf16[128,768]{1,0:T(8,128)(2,1)}) conditional(s32[]{:T(128)} %clamp.12, (bf16[128,768]{1,0:T(8,128)(2,1)}, bf16[128,768]{1,0:T(8,128)(2,1)}) %tuple.62, (bf16[128,768]{1,0:T(8,128)(2,1)}, bf16[128,768]{1,0:T(8,128)(2,1)}) %tuple.62, (bf16[128,768]{1,0:T(8,128)(2,1)}, ...), branch_computations={%region_6.6_spmd, %region_7.7_spmd, %region_8.8_spmd, %region_9.9_... | conditional | bytes 1572960 | solution.py:73
  144.5 42.7 %all-reduce.10.cloned.1.call-done = (f32[128,128]{1,0:T(8,128)}, f32[128,128]{1,0:T(8,128)}) async-done(((f32[128,128]{1,0:T(8,128)}, f32[128,128]{1,0:T(8,128)}), (f32[128,128]{1,0:T(8,128)}, f32[128,128]{1,0:T(8,128)})) %all-reduce.10.cloned.1.call-update) | async-done | bytes 131088 | tf_op jit(solution)/shard_map/while/body/eval_jaxpr/psum | solution.py:79
  204.5 40.7 %all-reduce.10.cloned.1.call-done = (f32[128,128]{1,0:T(8,128)}, f32[128,128]{1,0:T(8,128)}) async-done(((f32[128,128]{1,0:T(8,128)}, f32[128,128]{1,0:T(8,128)}), (f32[128,128]{1,0:T(8,128)}, f32[128,128]{1,0:T(8,128)})) %all-reduce.10.cloned.1.call-update) | async-done | bytes 131088 | tf_op jit(solution)/shard_map/while/body/eval_jaxpr/psum | solution.py:79
  268.2 41.8 %all-reduce.10.cloned.1.call-done = (f32[128,128]{1,0:T(8,128)}, f32[128,128]{1,0:T(8,128)}) async-done(((f32[128,128]{1,0:T(8,128)}, f32[128,128]{1,0:T(8,128)}), (f32[128,128]{1,0:T(8,128)}, f32[128,128]{1,0:T(8,128)})) %all-reduce.10.cloned.1.call-update) | async-done | bytes 131088 | tf_op jit(solution)/shard_map/while/body/eval_jaxpr/psum | solution.py:79
  327.3 40.7 %all-reduce.10.cloned.1.call-done = (f32[128,128]{1,0:T(8,128)}, f32[128,128]{1,0:T(8,128)}) async-done(((f32[128,128]{1,0:T(8,128)}, f32[128,128]{1,0:T(8,128)}), (f32[128,128]{1,0:T(8,128)}, f32[128,128]{1,0:T(8,128)})) %all-reduce.10.cloned.1.call-update) | async-done | bytes 131088 | tf_op jit(solution)/shard_map/while/body/eval_jaxpr/psum | solution.py:79
  371.9 13.1 %conditional.2 = (bf16[128,768]{1,0:T(8,128)(2,1)}, bf16[128,768]{1,0:T(8,128)(2,1)}) conditional(s32[]{:T(128)} %clamp.12, (bf16[128,768]{1,0:T(8,128)(2,1)}, bf16[128,768]{1,0:T(8,128)(2,1)}) %tuple.62, (bf16[128,768]{1,0:T(8,128)(2,1)}, bf16[128,768]{1,0:T(8,128)(2,1)}) %tuple.62, (bf16[128,768]{1,0:T(8,128)(2,1)}, ...), branch_computations={%region_6.6_spmd, %region_7.7_spmd, %region_8.8_spmd, %region_9.9_... | conditional | bytes 1572960 | solution.py:73
  391.7 42.7 %all-reduce.10.cloned.1.call-done = (f32[128,128]{1,0:T(8,128)}, f32[128,128]{1,0:T(8,128)}) async-done(((f32[128,128]{1,0:T(8,128)}, f32[128,128]{1,0:T(8,128)}), (f32[128,128]{1,0:T(8,128)}, f32[128,128]{1,0:T(8,128)})) %all-reduce.10.cloned.1.call-update) | async-done | bytes 131088 | tf_op jit(solution)/shard_map/while/body/eval_jaxpr/psum | solution.py:79
  451.7 40.7 %all-reduce.10.cloned.1.call-done = (f32[128,128]{1,0:T(8,128)}, f32[128,128]{1,0:T(8,128)}) async-done(((f32[128,128]{1,0:T(8,128)}, f32[128,128]{1,0:T(8,128)}), (f32[128,128]{1,0:T(8,128)}, f32[128,128]{1,0:T(8,128)})) %all-reduce.10.cloned.1.call-update) | async-done | bytes 131088 | tf_op jit(solution)/shard_map/while/body/eval_jaxpr/psum | solution.py:79
  496.2 21.5 %conditional.2 = (bf16[128,768]{1,0:T(8,128)(2,1)}, bf16[128,768]{1,0:T(8,128)(2,1)}) conditional(s32[]{:T(128)} %clamp.12, (bf16[128,768]{1,0:T(8,128)(2,1)}, bf16[128,768]{1,0:T(8,128)(2,1)}) %tuple.62, (bf16[128,768]{1,0:T(8,128)(2,1)}, bf16[128,768]{1,0:T(8,128)(2,1)}) %tuple.62, (bf16[128,768]{1,0:T(8,128)(2,1)}, ...), branch_computations={%region_6.6_spmd, %region_7.7_spmd, %region_8.8_spmd, %region_9.9_... | conditional | bytes 1572960 | solution.py:73
  524.5 42.0 %all-reduce.10.cloned.1.call-done = (f32[128,128]{1,0:T(8,128)}, f32[128,128]{1,0:T(8,128)}) async-done(((f32[128,128]{1,0:T(8,128)}, f32[128,128]{1,0:T(8,128)}), (f32[128,128]{1,0:T(8,128)}, f32[128,128]{1,0:T(8,128)})) %all-reduce.10.cloned.1.call-update) | async-done | bytes 131088 | tf_op jit(solution)/shard_map/while/body/eval_jaxpr/psum | solution.py:79
  583.9 40.7 %all-reduce.10.cloned.1.call-done = (f32[128,128]{1,0:T(8,128)}, f32[128,128]{1,0:T(8,128)}) async-done(((f32[128,128]{1,0:T(8,128)}, f32[128,128]{1,0:T(8,128)}), (f32[128,128]{1,0:T(8,128)}, f32[128,128]{1,0:T(8,128)})) %all-reduce.10.cloned.1.call-update) | async-done | bytes 131088 | tf_op jit(solution)/shard_map/while/body/eval_jaxpr/psum | solution.py:79
  628.4 13.1 %conditional.2 = (bf16[128,768]{1,0:T(8,128)(2,1)}, bf16[128,768]{1,0:T(8,128)(2,1)}) conditional(s32[]{:T(128)} %clamp.12, (bf16[128,768]{1,0:T(8,128)(2,1)}, bf16[128,768]{1,0:T(8,128)(2,1)}) %tuple.62, (bf16[128,768]{1,0:T(8,128)(2,1)}, bf16[128,768]{1,0:T(8,128)(2,1)}) %tuple.62, (bf16[128,768]{1,0:T(8,128)(2,1)}, ...), branch_computations={%region_6.6_spmd, %region_7.7_spmd, %region_8.8_spmd, %region_9.9_... | conditional | bytes 1572960 | solution.py:73
  648.2 42.7 %all-reduce.10.cloned.1.call-done = (f32[128,128]{1,0:T(8,128)}, f32[128,128]{1,0:T(8,128)}) async-done(((f32[128,128]{1,0:T(8,128)}, f32[128,128]{1,0:T(8,128)}), (f32[128,128]{1,0:T(8,128)}, f32[128,128]{1,0:T(8,128)})) %all-reduce.10.cloned.1.call-update) | async-done | bytes 131088 | tf_op jit(solution)/shard_map/while/body/eval_jaxpr/psum | solution.py:79
  708.3 40.7 %all-reduce.10.cloned.1.call-done = (f32[128,128]{1,0:T(8,128)}, f32[128,128]{1,0:T(8,128)}) async-done(((f32[128,128]{1,0:T(8,128)}, f32[128,128]{1,0:T(8,128)}), (f32[128,128]{1,0:T(8,128)}, f32[128,128]{1,0:T(8,128)})) %all-reduce.10.cloned.1.call-update) | async-done | bytes 131088 | tf_op jit(solution)/shard_map/while/body/eval_jaxpr/psum | solution.py:79
  752.8 12.4 %conditional.2 = (bf16[128,768]{1,0:T(8,128)(2,1)}, bf16[128,768]{1,0:T(8,128)(2,1)}) conditional(s32[]{:T(128)} %clamp.12, (bf16[128,768]{1,0:T(8,128)(2,1)}, bf16[128,768]{1,0:T(8,128)(2,1)}) %tuple.62, (bf16[128,768]{1,0:T(8,128)(2,1)}, bf16[128,768]{1,0:T(8,128)(2,1)}) %tuple.62, (bf16[128,768]{1,0:T(8,128)(2,1)}, ...), branch_computations={%region_6.6_spmd, %region_7.7_spmd, %region_8.8_spmd, %region_9.9_... | conditional | bytes 1572960 | solution.py:73
  771.9 41.8 %all-reduce.10.cloned.1.call-done = (f32[128,128]{1,0:T(8,128)}, f32[128,128]{1,0:T(8,128)}) async-done(((f32[128,128]{1,0:T(8,128)}, f32[128,128]{1,0:T(8,128)}), (f32[128,128]{1,0:T(8,128)}, f32[128,128]{1,0:T(8,128)})) %all-reduce.10.cloned.1.call-update) | async-done | bytes 131088 | tf_op jit(solution)/shard_map/while/body/eval_jaxpr/psum | solution.py:79
  831.1 40.7 %all-reduce.10.cloned.1.call-done = (f32[128,128]{1,0:T(8,128)}, f32[128,128]{1,0:T(8,128)}) async-done(((f32[128,128]{1,0:T(8,128)}, f32[128,128]{1,0:T(8,128)}), (f32[128,128]{1,0:T(8,128)}, f32[128,128]{1,0:T(8,128)})) %all-reduce.10.cloned.1.call-update) | async-done | bytes 131088 | tf_op jit(solution)/shard_map/while/body/eval_jaxpr/psum | solution.py:79
  875.6 13.1 %conditional.2 = (bf16[128,768]{1,0:T(8,128)(2,1)}, bf16[128,768]{1,0:T(8,128)(2,1)}) conditional(s32[]{:T(128)} %clamp.12, (bf16[128,768]{1,0:T(8,128)(2,1)}, bf16[128,768]{1,0:T(8,128)(2,1)}) %tuple.62, (bf16[128,768]{1,0:T(8,128)(2,1)}, bf16[128,768]{1,0:T(8,128)(2,1)}) %tuple.62, (bf16[128,768]{1,0:T(8,128)(2,1)}, ...), branch_computations={%region_6.6_spmd, %region_7.7_spmd, %region_8.8_spmd, %region_9.9_... | conditional | bytes 1572960 | solution.py:73
  895.5 42.7 %all-reduce.10.cloned.1.call-done = (f32[128,128]{1,0:T(8,128)}, f32[128,128]{1,0:T(8,128)}) async-done(((f32[128,128]{1,0:T(8,128)}, f32[128,128]{1,0:T(8,128)}), (f32[128,128]{1,0:T(8,128)}, f32[128,128]{1,0:T(8,128)})) %all-reduce.10.cloned.1.call-update) | async-done | bytes 131088 | tf_op jit(solution)/shard_map/while/body/eval_jaxpr/psum | solution.py:79
  955.5 40.7 %all-reduce.10.cloned.1.call-done = (f32[128,128]{1,0:T(8,128)}, f32[128,128]{1,0:T(8,128)}) async-done(((f32[128,128]{1,0:T(8,128)}, f32[128,128]{1,0:T(8,128)}), (f32[128,128]{1,0:T(8,128)}, f32[128,128]{1,0:T(8,128)})) %all-reduce.10.cloned.1.call-update) | async-done | bytes 131088 | tf_op jit(solution)/shard_map/while/body/eval_jaxpr/psum | solution.py:79
  1009.8 29.6 %reduce-scatter.2.cloned.1.call-done = f32[128,768]{1,0:T(8,128)} async-done(((f32[128,1536]{1,0:T(8,128)}), f32[128,768]{1,0:T(8,128)}) %reduce-scatter.2.cloned.1.call-update) | async-done | bytes 393232 | tf_op jit(solution)/shard_map/reduce_scatter | solution.py:108
  (217 shorter events, 398.1 us)
Async XLA Ops:
  7.2 57.2 %all-reduce.8.cloned.1.call-start = ((), (), s32[]{:S(2)}) async-start(), calls=%async_computation.1 | async-start | bytes 131072 | tf_op jit(solution)/shard_map/psum | solution.py:79
  66.6 54.2 %all-reduce.10.cloned.1.call-start = ((), (), s32[]{:S(2)}) async-start(), calls=%async_computation.3 | async-start | bytes 262144 | tf_op jit(solution)/shard_map/while/body/eval_jaxpr/psum | solution.py:79
  124.5 62.6 %all-reduce.10.cloned.1.call-start = ((), (), s32[]{:S(2)}) async-start(), calls=%async_computation.3 | async-start | bytes 262144 | tf_op jit(solution)/shard_map/while/body/eval_jaxpr/psum | solution.py:79
  124.6 9.0 collective-permute-start.2
  190.9 54.3 %all-reduce.10.cloned.1.call-start = ((), (), s32[]{:S(2)}) async-start(), calls=%async_computation.3 | async-start | bytes 262144 | tf_op jit(solution)/shard_map/while/body/eval_jaxpr/psum | solution.py:79
  248.9 61.1 %all-reduce.10.cloned.1.call-start = ((), (), s32[]{:S(2)}) async-start(), calls=%async_computation.3 | async-start | bytes 262144 | tf_op jit(solution)/shard_map/while/body/eval_jaxpr/psum | solution.py:79
  252.2 9.2 collective-permute-start.5
  313.7 54.3 %all-reduce.10.cloned.1.call-start = ((), (), s32[]{:S(2)}) async-start(), calls=%async_computation.3 | async-start | bytes 262144 | tf_op jit(solution)/shard_map/while/body/eval_jaxpr/psum | solution.py:79
  371.8 62.6 %all-reduce.10.cloned.1.call-start = ((), (), s32[]{:S(2)}) async-start(), calls=%async_computation.3 | async-start | bytes 262144 | tf_op jit(solution)/shard_map/while/body/eval_jaxpr/psum | solution.py:79
  371.9 9.0 collective-permute-start.2
  438.1 54.3 %all-reduce.10.cloned.1.call-start = ((), (), s32[]{:S(2)}) async-start(), calls=%async_computation.3 | async-start | bytes 262144 | tf_op jit(solution)/shard_map/while/body/eval_jaxpr/psum | solution.py:79
  496.1 70.4 %all-reduce.10.cloned.1.call-start = ((), (), s32[]{:S(2)}) async-start(), calls=%async_computation.3 | async-start | bytes 262144 | tf_op jit(solution)/shard_map/while/body/eval_jaxpr/psum | solution.py:79
  496.2 17.3 %collective-permute-start.6 = (bf16[128,768]{1,0:T(8,128)(2,1)}, bf16[128,768]{1,0:T(8,128)(2,1)}, u32[]{:S(2)}, u32[]{:S(2)}) collective-permute-start(bf16[128,768]{1,0:T(8,128)(2,1)} %get-tuple-element.277), channel_id=1, source_target_pairs={{0,16},{2,18},{4,20},{6,22},{8,24},{10,26},{12,28},{14,30},{16,0},... | collective-permute-start | bytes 589832 | tf_op jit(solution)/shard_map/while/body/eval_jaxpr/cond/branch_3_fun/ppermute | solution.py:16
  500.4 17.3 %collective-permute-start.7 = (bf16[128,768]{1,0:T(8,128)(2,1)}, bf16[128,768]{1,0:T(8,128)(2,1)}, u32[]{:S(2)}, u32[]{:S(2)}) collective-permute-start(bf16[128,768]{1,0:T(8,128)(2,1)} %get-tuple-element.278), channel_id=1, source_target_pairs={{0,16},{2,18},{4,20},{6,22},{8,24},{10,26},{12,28},{14,30},{16,0},... | collective-permute-start | bytes 589832 | tf_op jit(solution)/shard_map/while/body/eval_jaxpr/cond/branch_3_fun/ppermute | solution.py:16
  570.3 54.3 %all-reduce.10.cloned.1.call-start = ((), (), s32[]{:S(2)}) async-start(), calls=%async_computation.3 | async-start | bytes 262144 | tf_op jit(solution)/shard_map/while/body/eval_jaxpr/psum | solution.py:79
  628.3 62.6 %all-reduce.10.cloned.1.call-start = ((), (), s32[]{:S(2)}) async-start(), calls=%async_computation.3 | async-start | bytes 262144 | tf_op jit(solution)/shard_map/while/body/eval_jaxpr/psum | solution.py:79
  628.4 9.0 collective-permute-start.2
  694.6 54.3 %all-reduce.10.cloned.1.call-start = ((), (), s32[]{:S(2)}) async-start(), calls=%async_computation.3 | async-start | bytes 262144 | tf_op jit(solution)/shard_map/while/body/eval_jaxpr/psum | solution.py:79
  752.7 61.1 %all-reduce.10.cloned.1.call-start = ((), (), s32[]{:S(2)}) async-start(), calls=%async_computation.3 | async-start | bytes 262144 | tf_op jit(solution)/shard_map/while/body/eval_jaxpr/psum | solution.py:79
  756.0 9.2 collective-permute-start.5
  817.5 54.3 %all-reduce.10.cloned.1.call-start = ((), (), s32[]{:S(2)}) async-start(), calls=%async_computation.3 | async-start | bytes 262144 | tf_op jit(solution)/shard_map/while/body/eval_jaxpr/psum | solution.py:79
  875.5 62.6 %all-reduce.10.cloned.1.call-start = ((), (), s32[]{:S(2)}) async-start(), calls=%async_computation.3 | async-start | bytes 262144 | tf_op jit(solution)/shard_map/while/body/eval_jaxpr/psum | solution.py:79
  941.9 54.3 %all-reduce.10.cloned.1.call-start = ((), (), s32[]{:S(2)}) async-start(), calls=%async_computation.3 | async-start | bytes 262144 | tf_op jit(solution)/shard_map/while/body/eval_jaxpr/psum | solution.py:79
  999.9 39.5 %reduce-scatter.2.cloned.1.call-start = ((), (), s32[]{:S(2)}) async-start(), calls=%async_computation.2 | async-start | bytes 1179648 | tf_op jit(solution)/shard_map/reduce_scatter | solution.py:108
  (27 other events, 194.3 us)
Sparse Core Ops, SparseCore 0:
  16.2 48.1 all-reduce.7
  77.0 43.7 all-reduce.9
  141.4 45.7 all-reduce.9
  201.4 43.7 all-reduce.9
  265.1 44.8 all-reduce.9
  324.2 43.7 all-reduce.9
  388.6 45.7 all-reduce.9
  448.6 43.7 all-reduce.9
  521.4 45.1 all-reduce.9
  580.8 43.7 all-reduce.9
  645.1 45.7 all-reduce.9
  705.1 43.7 all-reduce.9
  768.8 44.8 all-reduce.9
  828.0 43.7 all-reduce.9
  892.3 45.7 all-reduce.9
  952.4 43.7 all-reduce.9
  1009.0 30.2 reduce-scatter.1
where the time goes:
time: 1050 us
  waiting for transfers between devices  766 us (73%)
  matrix products  116 us (11%)
  starting transfers between devices  84.3 us (8%)
  local copies, waits for them, and re-layouts  50.3 us (5%)
  between operations  15.1 us (1%)
    psum x16, waiting for transfers between devices, add_split(): lax.psum((inner_rows(img_unit, txt_block), inner_rows(img_block, txt_unit...  668 us
    ppermute x30, starting transfers between devices, from_partner(): return lax.ppermute(value, axis, pairs)  83.6 us
    ppermute x30, waiting for transfers between devices, from_partner(): return lax.ppermute(value, axis, pairs)  68.4 us
    dot_general x32, matrix products, inner_rows(): lax.dot_general(left, right, (((1,), (1,)), ((), ())), preferred_element_...  56.3 us
    while x30, local copies, waits for them, and re-layouts  48.4 us
    reduce_scatter x1, waiting for transfers between devices, local(): lax.psum_scatter(img_part, 'feat', scatter_dimension=1, tiled=True)  29.6 us
    dot_general x16, matrix products, inner_cols(): lax.dot_general(left, right, (((0,), (0,)), ((), ())), preferred_element_...  29.2 us
    dot_general x16, matrix products, add_split(): jnp.dot(first, txt_block, preferred_element_type=jnp.float32)  28.6 us
  transfers between devices with their start and end apart: 47, of which 39 were waited for; matrix products, arithmetic and copies ran while one was open for 5% of the time, Pallas kernels for 0%

commit v1 on v0

v1 whole, which is shorter than its diff:
```python
import functools

import jax
import jax.numpy as jnp
from jax import lax
from jax.experimental import pallas as pl
from jax.experimental.pallas import tpu as pltpu
from jax.sharding import PartitionSpec as P

EPS = 1e-06
MESH = pl.DeviceIdType.MESH
F32 = jnp.float32
BF16 = jnp.bfloat16
ROWS = 128
HALF = 64
LINE = 4


def dot_nt(left, right):
    return lax.dot_general(left, right, (((1,), (1,)), ((), ())), preferred_element_type=F32)


def dot_nn(left, right):
    return jnp.dot(left, right, preferred_element_type=F32)


def as_row(column):
    n = column.shape[0]
    return jnp.transpose(jnp.broadcast_to(column, (n, 128)))[0:8, :]


def as_column(row):
    n = row.shape[1]
    return jnp.transpose(jnp.broadcast_to(row, (128, n)))[:, 0:1]


def kernel(
    feats_hbm, text_hbm, proj_hbm, temp_ref, bias_ref, igrad_ref, tgrad_ref,
    feats, text, proj, iunit32, ibuf, traw, tbuf, tacc, tsend, tleft, tright, qacc, qsend, qrecv,
    rsend, rrecv, sq_out, sq_in, dot_out, dot_in, ipart, ipart_in, tpart, tpart_in,
    lsem, swap_s, swap_r, sq_s, sq_r, ig_s, ig_r, core_s, core_r, tf_right, tf_left, tf_r,
    tb_s, tb_left, tb_right, q_s, q_r, rs_s, rs_r, dot_s, dot_r, ip_s, ip_r, tp_s, tp_r,
):
    dp = lax.axis_index("dp")
    f = lax.axis_index("feat")
    zz = (dp // 4) % 4
    h = (dp // 2) % 2
    c = dp % 2
    core = (dp + 1 - 2 * c, f)
    near_a = (dp, 1 - f)
    near_b = (dp + 2 - 4 * h, 1 - f)
    z_up = (dp + 4, f)
    z_down = (dp - 4, f)
    has_up = zz < LINE - 1
    has_down = zz > 0

    def remote(src, dst, send, recv, to):
        return pltpu.make_async_remote_copy(
            src_ref=src, dst_ref=dst, send_sem=send, recv_sem=recv, device_id=to, device_id_type=MESH
        )

    sent = []

    def send(src, dst, s, r, to):
        copy = remote(src, dst, s, r, to)
        copy.start()
        sent.append(copy)

    def arrived(dst, r):
        remote(dst, dst, q_s.at[0], r, core).wait_recv()

    loads = [
        pltpu.make_async_copy(text_hbm, text, lsem.at[0]),
        pltpu.make_async_copy(feats_hbm, feats, lsem.at[1]),
        pltpu.make_async_copy(proj_hbm, proj, lsem.at[2]),
    ]
    for load in loads:
        load.start()

    barrier = pltpu.get_barrier_semaphore()
    for peer in (core, near_a, near_b):
        pl.semaphore_signal(barrier, inc=1, device_id=peer, device_id_type=MESH)

    @pl.when(has_up)
    def _():
        pl.semaphore_signal(barrier, inc=1, device_id=z_up, device_id_type=MESH)

    @pl.when(has_down)
    def _():
        pl.semaphore_signal(barrier, inc=1, device_id=z_down, device_id_type=MESH)

    pl.semaphore_wait(barrier, 3 + has_up.astype(jnp.int32) + has_down.astype(jnp.int32))

    scale = jnp.exp(jnp.full((1, 1), temp_ref[0], F32))
    offset = bias_ref[0]

    loads[0].wait()
    theirs = pl.multiple_of(HALF * (1 - f), HALF)
    mine = pl.multiple_of(HALF * f, HALF)
    send(text.at[pl.ds(theirs, HALF)], traw.at[f], swap_s.at[0], swap_r.at[0], near_a)
    traw[f] = text[pl.ds(mine, HALF), :]

    loads[1].wait()
    loads[2].wait()
    emb = dot_nn(feats[...], proj[...])
    iunit32[...] = emb
    sq_out[...] = as_row(jnp.sum(emb * emb, axis=1, keepdims=True))
    send(sq_out, sq_in, sq_s.at[0], sq_r.at[0], near_a)

    arrived(traw.at[1 - f], swap_r.at[0])
    t0 = traw[0].astype(F32)
    t1 = traw[1].astype(F32)
    tnorm = jnp.sqrt(jnp.sum(t0 * t0 + t1 * t1, axis=1, keepdims=True) + EPS)
    own_t = pl.ds(pl.multiple_of(zz * HALF, HALF), HALF)
    tbuf[0, own_t] = (t0 / tnorm).astype(BF16)
    tbuf[1, own_t] = (t1 / tnorm).astype(BF16)

    line_copies = []

    def block(ref, e, b):
        return ref.at[e, pl.ds(pl.multiple_of(b * HALF, HALF), HALF)]

    def t_forward(dist):
        for sign, can, to, sems in ((-1, has_up, z_up, tf_right), (1, has_down, z_down, tf_left)):
            b = zz + sign * dist
            here = (b >= 0) if sign < 0 else (b < LINE)

            @pl.when(here)
            def _():
                for e in range(2):
                    if dist > 0:
                        arrived(block(tbuf, e, b), tf_r.at[b, e])

                    @pl.when(can)
                    def _():
                        remote(block(tbuf, e, b), block(tbuf, e, b), sems.at[dist, e], tf_r.at[b, e], to).start()

    def t_forward_sent(dist):
        for sign, can, to, sems in ((-1, has_up, z_up, tf_right), (1, has_down, z_down, tf_left)):
            b = zz + sign * dist
            here = (b >= 0) if sign < 0 else (b < LINE)

            @pl.when(jnp.logical_and(here, can))
            def _():
                for e in range(2):
                    remote(block(tbuf, e, b), block(tbuf, e, b), sems.at[dist, e], tf_r.at[b, e], to).wait_send()

    t_forward(0)

    arrived(sq_in, sq_r.at[0])
    inorm = jnp.sqrt(as_column(sq_out[0:1, :] + sq_in[0:1, :]) + EPS)
    unit32 = iunit32[...] / inorm
    iunit32[...] = unit32

    def img(width, core_at, high, part=None):
        start = (core_at * 2 + high) * ROWS + (0 if part is None else part * HALF)
        size = ROWS if part is None else HALF
        return ibuf.at[width, pl.ds(pl.multiple_of(start, HALF), size)]

    ibuf[f, pl.ds(pl.multiple_of((c * 2 + h) * ROWS, ROWS), ROWS)] = unit32.astype(BF16)

    def give(part_ref, slot, to):
        send(part_ref, part_ref, ig_s.at[slot], ig_r.at[slot], to)

    give(img(f, c, h, 0), 0, near_a)
    give(img(f, c, h, 1), 3, near_b)
    give(img(f, c, h, 1), 1, near_a)
    give(img(f, c, h, 0), 2, near_b)

    def share(piece, slot):
        send(piece, piece, core_s.at[slot], core_r.at[slot], core)

    share(img(f, c, h), 0)
    t_forward(1)
    arrived(img(1 - f, c, h, 0), ig_r.at[0])
    give(img(1 - f, c, h, 0), 4, near_b)
    arrived(img(1 - f, c, 1 - h, 1), ig_r.at[3])
    give(img(1 - f, c, 1 - h, 1), 5, near_a)
    arrived(img(1 - f, c, h, 1), ig_r.at[1])
    share(img(1 - f, c, h), 1)
    arrived(img(1 - f, c, 1 - h, 0), ig_r.at[2])
    share(img(1 - f, c, 1 - h), 2)
    t_forward(2)
    arrived(img(f, c, 1 - h, 0), ig_r.at[4])
    arrived(img(f, c, 1 - h, 1), ig_r.at[5])
    share(img(f, c, 1 - h), 3)
    t_forward(3)
    arrived(img(f, 1 - c, h), core_r.at[0])
    arrived(img(1 - f, 1 - c, h), core_r.at[1])
    arrived(img(1 - f, 1 - c, 1 - h), core_r.at[2])
    arrived(img(f, 1 - c, 1 - h), core_r.at[3])

    sums = dot_nt(ibuf[0], tbuf[0]) + dot_nt(ibuf[1], tbuf[1])
    logits = scale * sums + offset
    row = lax.broadcasted_iota(jnp.int32, logits.shape, 0) - ((c * 2 + h) * ROWS + mine)
    col = lax.broadcasted_iota(jnp.int32, logits.shape, 1) - zz * HALF
    same = jnp.logical_and(row == col, jnp.logical_and(col >= 0, col < HALF))
    weights32 = jax.nn.sigmoid(logits) - jnp.where(same, 1.0, 0.0)
    weights = weights32.astype(BF16)
    weights_t = jnp.transpose(weights32).astype(BF16)

    for e in range(2):
        tacc[e] = scale * dot_nn(weights_t, ibuf[e])

    def t_back(dist):
        for sign, can, to, inbox, r, there in (
            (-1, has_up, z_down, tright, tb_right, has_down),
            (1, has_down, z_up, tleft, tb_left, has_up),
        ):
            b = zz + sign * dist
            here = (b >= 0) if sign < 0 else (b < LINE)

            @pl.when(here)
            def _():
                at = pl.ds(pl.multiple_of(b * HALF, HALF), HALF)
                for e in range(2):

                    @pl.when(can)
                    def _():
                        arrived(inbox.at[e, at], r.at[b, e])
                        tsend[e, at] = (tacc[e, at] + inbox[e, at].astype(F32)).astype(BF16)

                    @pl.when(jnp.logical_not(can))
                    def _():
                        tsend[e, at] = tacc[e, at].astype(BF16)

                    remote(tsend.at[e, at], inbox.at[e, at], tb_s.at[b, e], r.at[b, e], to).start()

    def t_back_sent(dist):
        for sign, to, inbox, r in ((-1, z_down, tright, tb_right), (1, z_up, tleft, tb_left)):
            b = zz + sign * dist
            here = (b >= 0) if sign < 0 else (b < LINE)

            @pl.when(here)
            def _():
                at = pl.ds(pl.multiple_of(b * HALF, HALF), HALF)
                for e in range(2):
                    remote(tsend.at[e, at], inbox.at[e, at], tb_s.at[b, e], r.at[b, e], to).wait_send()

    t_back(3)

    other = pl.ds(pl.multiple_of((1 - c) * 2 * ROWS, ROWS), 2 * ROWS)
    own = pl.ds(pl.multiple_of(c * 2 * ROWS, ROWS), 2 * ROWS)
    for e in range(2):
        qacc[e] = scale * dot_nn(weights, tbuf[e])
        qsend[e] = qacc[e, other].astype(BF16)
        send(qsend.at[e], qrecv.at[e], q_s.at[e], q_r.at[e], core)

    t_back(2)

    def quarter(width, high, part):
        start = (c * 2 + high) * ROWS + part * HALF
        return width, pl.ds(pl.multiple_of(start, HALF), HALF)

    for e in range(2):
        arrived(qrecv.at[e], q_r.at[e])
        qacc[e, own] = qacc[e, own] + qrecv[e].astype(F32)

    def hand(slot, value, to):
        rsend[slot] = value.astype(BF16)
        send(rsend.at[slot], rrecv.at[slot], rs_s.at[slot], rs_r.at[slot], to)

    def got(slot):
        arrived(rrecv.at[slot], rs_r.at[slot])
        return rrecv[slot].astype(F32)

    hand(0, qacc[quarter(f, 1 - h, 0)], near_a)
    hand(1, qacc[quarter(f, 1 - h, 1)], near_b)
    hand(2, qacc[quarter(1 - f, h, 0)], near_a)
    hand(5, qacc[quarter(1 - f, 1 - h, 1)], near_b)
    t_back(1)
    hand(4, qacc[quarter(1 - f, 1 - h, 0)] + got(0), near_b)
    hand(3, qacc[quarter(1 - f, h, 1)] + got(1), near_a)

    for e in range(2):

        @pl.when(has_down)
        def _():
            arrived(block(tleft, e, zz), tb_left.at[zz, e])
            tacc[e, own_t] = tacc[e, own_t] + tleft[e, own_t].astype(F32)

        @pl.when(has_up)
        def _():
            arrived(block(tright, e, zz), tb_right.at[zz, e])
            tacc[e, own_t] = tacc[e, own_t] + tright[e, own_t].astype(F32)

    u0 = traw[0].astype(F32) / tnorm
    u1 = traw[1].astype(F32) / tnorm
    b0 = tacc[0, own_t]
    b1 = tacc[1, own_t]
    tdot = jnp.sum(u0 * b0 + u1 * b1, axis=1, keepdims=True)
    tacc[0, own_t] = (b0 - u0 * tdot) / tnorm
    tacc[1, own_t] = (b1 - u1 * tdot) / tnorm
    tpart[...] = tacc[1 - f, own_t].astype(BF16)
    send(tpart, tpart_in, tp_s.at[0], tp_r.at[0], near_a)
    tgrad_ref[pl.ds(mine, HALF), :] = tacc[f, own_t]

    low = qacc[quarter(f, h, 0)] + got(2) + got(4)
    high = qacc[quarter(f, h, 1)] + got(3) + got(5)
    back = jnp.concatenate([low, high], axis=0)
    unit = iunit32[...]
    dot_out[...] = as_row(jnp.sum(unit * back, axis=1, keepdims=True))
    send(dot_out, dot_in, dot_s.at[0], dot_r.at[0], near_a)
    arrived(dot_in, dot_r.at[0])
    idot = as_column(dot_out[0:1, :] + dot_in[0:1, :])
    direction = ((back - unit * idot) / inorm).astype(BF16)
    width = proj.shape[1]
    theirs_h = pl.ds(pl.multiple_of((1 - f) * width, width), width)
    mine_h = pl.ds(pl.multiple_of(f * width, width), width)
    ipart[...] = dot_nt(direction, proj[theirs_h, :]).astype(BF16)
    send(ipart, ipart_in, ip_s.at[0], ip_r.at[0], near_a)
    ours = dot_nt(direction, proj[mine_h, :])

    arrived(tpart_in, tp_r.at[0])
    tgrad_ref[pl.ds(theirs, HALF), :] = tpart_in[...].astype(F32)
    arrived(ipart_in, ip_r.at[0])
    igrad_ref[...] = ours + ipart_in[...].astype(F32)

    for copy in sent:
        copy.wait_send()
    for dist in range(LINE):
        t_forward_sent(dist)
        if dist > 0:
            t_back_sent(dist)


def local(image_feats, text_emb, image_proj, log_temp, bias):
    rows, wide = image_feats.shape
    width = text_emb.shape[1]
    dma = pltpu.SemaphoreType.DMA
    group = 4 * rows
    text_rows = LINE * HALF
    return pl.pallas_call(
        kernel,
        out_shape=(jax.ShapeDtypeStruct((rows, width), F32), jax.ShapeDtypeStruct((rows, width), F32)),
        in_specs=[pl.BlockSpec(memory_space=pl.ANY)] * 3 + [pl.BlockSpec(memory_space=pltpu.SMEM)] * 2,
        out_specs=(pl.BlockSpec(memory_space=pltpu.VMEM), pl.BlockSpec(memory_space=pltpu.VMEM)),
        scratch_shapes=[
            pltpu.VMEM((rows, wide), BF16),
            pltpu.VMEM((rows, width), BF16),
            pltpu.VMEM((wide, width), BF16),
            pltpu.VMEM((rows, width), F32),
            pltpu.VMEM((2, group, width), BF16),
            pltpu.VMEM((2, HALF, width), BF16),
            pltpu.VMEM((2, text_rows, width), BF16),
            pltpu.VMEM((2, text_rows, width), F32),
            pltpu.VMEM((2, text_rows, width), BF16),
            pltpu.VMEM((2, text_rows, width), BF16),
            pltpu.VMEM((2, text_rows, width), BF16),
            pltpu.VMEM((2, group, width), F32),
            pltpu.VMEM((2, 2 * rows, width), BF16),
            pltpu.VMEM((2, 2 * rows, width), BF16),
            pltpu.VMEM((6, HALF, width), BF16),
            pltpu.VMEM((6, HALF, width), BF16),
            pltpu.VMEM((8, rows), F32),
            pltpu.VMEM((8, rows), F32),
            pltpu.VMEM((8, rows), F32),
            pltpu.VMEM((8, rows), F32),
            pltpu.VMEM((rows, width), BF16),
            pltpu.VMEM((rows, width), BF16),
            pltpu.VMEM((HALF, width), BF16),
            pltpu.VMEM((HALF, width), BF16),
            dma((3,)),
            dma((1,)), dma((1,)),
            dma((1,)), dma((1,)),
            dma((6,)), dma((6,)),
            dma((4,)), dma((4,)),
            dma((4, 2)), dma((4, 2)), dma((4, 2)),
            dma((4, 2)), dma((4, 2)), dma((4, 2)),
            dma((2,)), dma((2,)),
            dma((6,)), dma((6,)),
            dma((1,)), dma((1,)),
            dma((1,)), dma((1,)),
            dma((1,)), dma((1,)),
        ],
        compiler_params=pltpu.CompilerParams(
            collective_id=0, has_side_effects=True, vmem_limit_bytes=48 << 20
        ),
        name="contrastive_backward",
    )(image_feats, text_emb, image_proj, log_temp, bias)


def solution(mesh):
    placed = (P("dp", None), P("dp", "feat"), P(None, "feat"), P(), P())
    return jax.shard_map(
        local,
        mesh=mesh,
        in_specs=placed,
        out_specs=(P("dp", "feat"), P("dp", "feat")),
        check_vma=False,
    )
```

time: 1050 us -> 60.3 us (0.06)
  the two profiles are of different devices: /device:TPU:1 before, /device:TPU:32 now
where the time goes in v1:
time: 60.3 us; the launch traced here: 60.1 us
  Pallas kernels  53.1 us (88%)
  local copies, waits for them, and re-layouts  5.07 us (8%)
  between operations  1.94 us (3%)
    pallas_call x1, Pallas kernels, local(): pl.pallas_call(kernel, out_shape=(jax.ShapeDtypeStruct((rows, width), F32...  53.1 us
    unnamed x8, local copies, waits for them, and re-layouts  5.07 us

profile of v1, /device:TPU:32, one launch (start us, length us, event | category | flops | bytes accessed | tf_op | source)
XLA Modules:
  0.0 60.1 jit_solution(14932171382214244164)
XLA Ops:
  1.9 0.0 copy-start
  1.9 1.7 %copy-done = bf16[1536,768]{1,0:T(8,128)(2,1)S(1)} copy-done((bf16[1536,768]{1,0:T(8,128)(2,1)S(1)}, bf16[1536,768]{1,0:T(8,128)(2,1)}, u32[]{:S(2)}) %copy-start) | copy-done | bytes 2359320
  3.6 0.0 copy-start.1
  3.6 1.0 %copy-done.1 = bf16[128,1536]{1,0:T(8,128)(2,1)S(1)} copy-done((bf16[128,1536]{1,0:T(8,128)(2,1)S(1)}, bf16[128,1536]{1,0:T(8,128)(2,1)}, u32[]{:S(2)}) %copy-start.1) | copy-done | bytes 393240
  4.6 0.0 copy-start.2
  4.6 0.9 %copy-done.2 = bf16[128,768]{1,0:T(8,128)(2,1)S(1)} copy-done((bf16[128,768]{1,0:T(8,128)(2,1)S(1)}, bf16[128,768]{1,0:T(8,128)(2,1)}, u32[]{:S(2)}) %copy-start.2) | copy-done | bytes 196632
  5.5 53.1 %contrastive_backward.1 = (f32[128,768]{1,0:T(8,128)S(1)}, f32[128,768]{1,0:T(8,128)S(1)}) custom-call(bf16[128,1536]{1,0:T(8,128)(2,1)S(1)} %copy-done.1, bf16[128,768]{1,0:T(8,128)(2,1)S(1)} %copy-done.2, bf16[1536,768]{1,0:T(8,128)(2,1)S(1)} %copy-done, f32[1]{0:T(128)S(6)} %copy.9.temp_ref, f32[1]{0:T(128)S(6)} %copy.10.bias_ref), custom_call_target="tpu_custom_call" | custom-call | tf_op jit(solution)/shard_map/contrastive_backward/pallas_call | solution.py:333
  58.6 0.7 %copy.11 = f32[128,768]{1,0:T(8,128)} copy(f32[128,768]{1,0:T(8,128)S(1)} %get-tuple-element.4) | data formatting | bytes 786432
  59.3 0.7 %copy.12 = f32[128,768]{1,0:T(8,128)} copy(f32[128,768]{1,0:T(8,128)S(1)} %get-tuple-element.5) | data formatting | bytes 786432
Async XLA Ops:
  1.9 1.7 %copy-start = (bf16[1536,768]{1,0:T(8,128)(2,1)S(1)}, bf16[1536,768]{1,0:T(8,128)(2,1)}, u32[]{:S(2)}) copy-start(bf16[1536,768]{1,0:T(8,128)(2,1)} %proj_hbm.1) | copy-start | bytes 7077892
  3.6 1.0 %copy-start.1 = (bf16[128,1536]{1,0:T(8,128)(2,1)S(1)}, bf16[128,1536]{1,0:T(8,128)(2,1)}, u32[]{:S(2)}) copy-start(bf16[128,1536]{1,0:T(8,128)(2,1)} %feats_hbm.1) | copy-start | bytes 1179652
  4.6 0.9 %copy-start.2 = (bf16[128,768]{1,0:T(8,128)(2,1)S(1)}, bf16[128,768]{1,0:T(8,128)(2,1)}, u32[]{:S(2)}) copy-start(bf16[128,768]{1,0:T(8,128)(2,1)} %text_hbm.1) | copy-start | bytes 589828

commit v2 on v1

v2 whole, which is shorter than its diff:
```python
import functools

import jax
import jax.numpy as jnp
from jax import lax
from jax.experimental import pallas as pl
from jax.experimental.pallas import tpu as pltpu
from jax.sharding import PartitionSpec as P

EPS = 1e-06
MESH = pl.DeviceIdType.MESH
F32 = jnp.float32
BF16 = jnp.bfloat16
ROWS = 128
HALF = 64
LINE = 4


def dot_nt(left, right):
    return lax.dot_general(left, right, (((1,), (1,)), ((), ())), preferred_element_type=F32)


def dot_nn(left, right):
    return jnp.dot(left, right, preferred_element_type=F32)


def as_row(column):
    n = column.shape[0]
    return jnp.transpose(jnp.broadcast_to(column, (n, 128)))[0:8, :]


def as_column(row):
    n = row.shape[1]
    return jnp.transpose(jnp.broadcast_to(row, (128, n)))[:, 0:1]


def kernel(
    feats_hbm, text_hbm, proj_hbm, temp_ref, bias_ref, igrad_ref, tgrad_ref,
    feats, text, proj, iunit32, ibuf, tbuf, tunit, tnorms, tacc, tsend, tleft, tright, qacc, qsend, qrecv,
    rsend, rrecv, sq_out, sq_in, dots, dot_all, dot_core, dot_out, dot_in, ipart, ipart_in, tpart, tpart_in,
    lsem, sq_s, sq_r, ig_s, ig_r, core_s, core_r, tf_swap, tf_up, tf_down, tf_r,
    tb_s, tb_left, tb_right, q_s, q_r, rs_s, rs_r, dc_s, dc_r, dot_s, dot_r, ip_s, ip_r, tp_s, tp_r,
):
    dp = lax.axis_index("dp")
    f = lax.axis_index("feat")
    zz = (dp // 4) % 4
    h = (dp // 2) % 2
    c = dp % 2
    opposite = dp + 2 - 4 * h
    core = (dp + 1 - 2 * c, f)
    near_a = (dp, 1 - f)
    near_b = (opposite, 1 - f)
    far = (opposite, f)
    z_up = (dp + 4, f)
    z_down = (dp - 4, f)
    has_up = zz < LINE - 1
    has_down = zz > 0

    def remote(src, dst, send, recv, to):
        return pltpu.make_async_remote_copy(
            src_ref=src, dst_ref=dst, send_sem=send, recv_sem=recv, device_id=to, device_id_type=MESH
        )

    sent = []

    def send(src, dst, s, r, to):
        copy = remote(src, dst, s, r, to)
        copy.start()
        sent.append(copy)

    def arrived(dst, r):
        remote(dst, dst, q_s.at[0], r, core).wait_recv()

    loads = [
        pltpu.make_async_copy(text_hbm, text, lsem.at[0]),
        pltpu.make_async_copy(feats_hbm, feats, lsem.at[1]),
        pltpu.make_async_copy(proj_hbm, proj, lsem.at[2]),
    ]
    for load in loads:
        load.start()

    barrier = pltpu.get_barrier_semaphore()
    for peer in (core, near_a, near_b, far):
        pl.semaphore_signal(barrier, inc=1, device_id=peer, device_id_type=MESH)

    @pl.when(has_up)
    def _():
        pl.semaphore_signal(barrier, inc=1, device_id=z_up, device_id_type=MESH)

    @pl.when(has_down)
    def _():
        pl.semaphore_signal(barrier, inc=1, device_id=z_down, device_id_type=MESH)

    loads[0].wait()
    pl.semaphore_wait(barrier, 4 + has_up.astype(jnp.int32) + has_down.astype(jnp.int32))

    scale = jnp.exp(jnp.full((1, 1), temp_ref[0], F32))
    offset = bias_ref[0]

    theirs = pl.ds(pl.multiple_of(HALF * (1 - f), HALF), HALF)
    mine = pl.ds(pl.multiple_of(HALF * f, HALF), HALF)

    def rows_of(b):
        return pl.ds(pl.multiple_of(b * HALF, HALF), HALF)

    def block(ref, e, b):
        return ref.at[e, rows_of(b)]

    own_t = rows_of(zz)
    send(text.at[theirs], block(tbuf, f, zz), tf_swap.at[0], tf_r.at[zz, f], near_a)

    def t_forward(dist, e, src=None):
        for sign, can, to, sems in ((-1, has_up, z_up, tf_up), (1, has_down, z_down, tf_down)):
            b = zz + sign * dist
            here = (b >= 0) if sign < 0 else (b < LINE)

            @pl.when(here)
            def _():
                if dist > 0:
                    arrived(block(tbuf, e, b), tf_r.at[b, e])

                @pl.when(can)
                def _():
                    origin = block(tbuf, e, b) if src is None else src
                    remote(origin, block(tbuf, e, b), sems.at[dist, e], tf_r.at[b, e], to).start()

    def t_forward_sent(dist, e):
        for sign, can, to, sems in ((-1, has_up, z_up, tf_up), (1, has_down, z_down, tf_down)):
            b = zz + sign * dist
            here = (b >= 0) if sign < 0 else (b < LINE)

            @pl.when(jnp.logical_and(here, can))
            def _():
                remote(block(tbuf, e, b), block(tbuf, e, b), sems.at[dist, e], tf_r.at[b, e], to).wait_send()

    def normalise(b):
        at = rows_of(b)
        t0 = tbuf[0, at].astype(F32)
        t1 = tbuf[1, at].astype(F32)
        norm = jnp.sqrt(jnp.sum(t0 * t0 + t1 * t1, axis=1, keepdims=True) + EPS)
        tnorms[at] = jnp.broadcast_to(norm, (HALF, 128))
        tunit[0, at] = (t0 / norm).astype(BF16)
        tunit[1, at] = (t1 / norm).astype(BF16)

    def normalise_at(dist):
        for b, here in ((zz - dist, zz - dist >= 0), (zz + dist, zz + dist < LINE)):

            @pl.when(here)
            def _():
                normalise(b)

    t_forward(0, f, text.at[mine])
    tbuf[f, own_t] = text[mine, :]

    loads[1].wait()
    loads[2].wait()
    emb = dot_nn(feats[...], proj[...])
    iunit32[...] = emb
    sq_out[...] = as_row(jnp.sum(emb * emb, axis=1, keepdims=True))
    send(sq_out, sq_in, sq_s.at[0], sq_r.at[0], near_a)

    arrived(block(tbuf, 1 - f, zz), tf_r.at[zz, 1 - f])
    t_forward(0, 1 - f)
    normalise(zz)

    arrived(sq_in, sq_r.at[0])
    inorm = jnp.sqrt(as_column(sq_out[0:1, :] + sq_in[0:1, :]) + EPS)
    unit32 = iunit32[...] / inorm
    iunit32[...] = unit32

    def img(width, core_at, high, part=None):
        start = (core_at * 2 + high) * ROWS + (0 if part is None else part * HALF)
        size = ROWS if part is None else HALF
        return ibuf.at[width, pl.ds(pl.multiple_of(start, HALF), size)]

    ibuf[f, pl.ds(pl.multiple_of((c * 2 + h) * ROWS, ROWS), ROWS)] = unit32.astype(BF16)

    def give(part_ref, slot, to):
        send(part_ref, part_ref, ig_s.at[slot], ig_r.at[slot], to)

    give(img(f, c, h, 0), 0, near_a)
    give(img(f, c, h, 1), 3, near_b)
    give(img(f, c, h, 1), 1, near_a)
    give(img(f, c, h, 0), 2, near_b)

    def share(piece, slot):
        send(piece, piece, core_s.at[slot], core_r.at[slot], core)

    share(img(f, c, h), 0)
    t_forward(1, f)
    t_forward(1, 1 - f)
    arrived(img(1 - f, c, h, 0), ig_r.at[0])
    give(img(1 - f, c, h, 0), 4, near_b)
    arrived(img(1 - f, c, 1 - h, 1), ig_r.at[3])
    give(img(1 - f, c, 1 - h, 1), 5, near_a)
    normalise_at(1)
    arrived(img(1 - f, c, h, 1), ig_r.at[1])
    share(img(1 - f, c, h), 1)
    arrived(img(1 - f, c, 1 - h, 0), ig_r.at[2])
    share(img(1 - f, c, 1 - h), 2)
    t_forward(2, f)
    t_forward(2, 1 - f)
    normalise_at(2)
    arrived(img(f, c, 1 - h, 0), ig_r.at[4])
    arrived(img(f, c, 1 - h, 1), ig_r.at[5])
    share(img(f, c, 1 - h), 3)
    t_forward(3, f)
    t_forward(3, 1 - f)
    normalise_at(3)
    arrived(img(f, 1 - c, h), core_r.at[0])
    arrived(img(1 - f, 1 - c, h), core_r.at[1])
    arrived(img(1 - f, 1 - c, 1 - h), core_r.at[2])
    arrived(img(f, 1 - c, 1 - h), core_r.at[3])

    sums = dot_nt(ibuf[0], tunit[0]) + dot_nt(ibuf[1], tunit[1])
    logits = scale * sums + offset
    row = lax.broadcasted_iota(jnp.int32, logits.shape, 0) - ((c * 2 + h) * ROWS + HALF * f)
    col = lax.broadcasted_iota(jnp.int32, logits.shape, 1) - zz * HALF
    same = jnp.logical_and(row == col, jnp.logical_and(col >= 0, col < HALF))
    weights32 = jax.nn.sigmoid(logits) - jnp.where(same, 1.0, 0.0)
    weights = weights32.astype(BF16)
    weights_t = jnp.transpose(weights32).astype(BF16)

    for e in range(2):
        tacc[e] = dot_nn(weights_t, ibuf[e])

    def t_back(dist):
        for e in range(2):
            for sign, can, to, inbox, r in (
                (-1, has_up, z_down, tright, tb_right),
                (1, has_down, z_up, tleft, tb_left),
            ):
                b = zz + sign * dist
                here = (b >= 0) if sign < 0 else (b < LINE)

                @pl.when(here)
                def _():
                    at = rows_of(b)

                    @pl.when(can)
                    def _():
                        arrived(inbox.at[e, at], r.at[b, e])
                        tsend[e, at] = (tacc[e, at] + inbox[e, at].astype(F32)).astype(BF16)

                    @pl.when(jnp.logical_not(can))
                    def _():
                        tsend[e, at] = tacc[e, at].astype(BF16)

                    remote(tsend.at[e, at], inbox.at[e, at], tb_s.at[b, e], r.at[b, e], to).start()

    def t_back_sent(dist):
        for sign, to, inbox, r in ((-1, z_down, tright, tb_right), (1, z_up, tleft, tb_left)):
            b = zz + sign * dist
            here = (b >= 0) if sign < 0 else (b < LINE)

            @pl.when(here)
            def _():
                at = rows_of(b)
                for e in range(2):
                    remote(tsend.at[e, at], inbox.at[e, at], tb_s.at[b, e], r.at[b, e], to).wait_send()

    t_back(3)

    def quarter(core_at, high, part=None):
        start = (core_at * 2 + high) * ROWS + (0 if part is None else part * HALF)
        return pl.ds(pl.multiple_of(start, HALF), ROWS if part is None else HALF)

    rows_other = pl.ds(pl.multiple_of((1 - c) * 2 * ROWS, ROWS), 2 * ROWS)
    rows_own = pl.ds(pl.multiple_of(c * 2 * ROWS, ROWS), 2 * ROWS)
    wide_weights = dots
    wide_weights[...] = weights
    order = ((f, 1 - h), (1 - f, 1 - h), (1 - f, h), (f, h))
    for slot, (width, high) in enumerate(order):
        qsend[slot] = dot_nn(wide_weights[quarter(1 - c, high), :], tunit[width]).astype(BF16)
        send(qsend.at[slot], qrecv.at[slot], q_s.at[slot], q_r.at[slot], core)

    part = jnp.sum(weights32 * sums, axis=1, keepdims=True)
    dot_all[...] = as_row(part)
    ds_other = pl.ds(pl.multiple_of((1 - c) * 2 * ROWS, ROWS), 2 * ROWS)
    ds_own = pl.ds(pl.multiple_of(c * 2 * ROWS, ROWS), 2 * ROWS)
    dot_core[0] = dot_all[:, ds_other]
    send(dot_core.at[0], dot_core.at[1], dc_s.at[0], dc_r.at[0], core)

    for e in range(2):
        qacc[e] = dot_nn(wide_weights[rows_own, :], tunit[e])

    def mid(high, part):
        return pl.ds(pl.multiple_of(high * ROWS + part * HALF, HALF), HALF)

    def whole(slot, width, high):
        arrived(qrecv.at[slot], q_r.at[slot])
        at = pl.ds(pl.multiple_of(high * ROWS, ROWS), ROWS)
        qacc[width, at] = qacc[width, at] + qrecv[slot].astype(F32)

    def hand(slot, value, to):
        rsend[slot] = value.astype(BF16)
        send(rsend.at[slot], rrecv.at[slot], rs_s.at[slot], rs_r.at[slot], to)

    def got(slot):
        arrived(rrecv.at[slot], rs_r.at[slot])
        return rrecv[slot].astype(F32)

    whole(0, f, 1 - h)
    hand(0, qacc[f, mid(1 - h, 0)], near_a)
    hand(1, qacc[f, mid(1 - h, 1)], near_b)
    whole(1, 1 - f, 1 - h)
    hand(5, qacc[1 - f, mid(1 - h, 1)], near_b)
    whole(2, 1 - f, h)
    hand(2, qacc[1 - f, mid(h, 0)], near_a)
    arrived(dot_core.at[1], dc_r.at[0])
    dot_core[2] = dot_all[:, ds_own] + dot_core[1]
    for slot, high, to in ((0, h, near_a), (1, 1 - h, near_b), (2, 1 - h, far)):
        dot_out[slot] = dot_core[2, :, pl.ds(pl.multiple_of(high * ROWS, ROWS), ROWS)]
        send(dot_out.at[slot], dot_in.at[slot], dot_s.at[slot], dot_r.at[slot], to)
    whole(3, f, h)
    t_back(2)
    hand(4, qacc[1 - f, mid(1 - h, 0)] + got(0), near_b)
    hand(3, qacc[1 - f, mid(h, 1)] + got(1), near_a)
    t_back(1)

    for slot in range(3):
        arrived(dot_in.at[slot], dot_r.at[slot])
    idot_row = dot_core[2, 0:1, pl.ds(pl.multiple_of(h * ROWS, ROWS), ROWS)]
    idot = as_column(idot_row + dot_in[0, 0:1, :] + dot_in[1, 0:1, :] + dot_in[2, 0:1, :])
    low = qacc[f, mid(h, 0)] + got(2) + got(4)
    high = qacc[f, mid(h, 1)] + got(5) + got(3)
    back = jnp.concatenate([low, high], axis=0)
    direction = ((back - iunit32[...] * idot) * (scale / inorm)).astype(BF16)
    width = proj.shape[1]
    theirs_h = pl.ds(pl.multiple_of((1 - f) * width, width), width)
    mine_h = pl.ds(pl.multiple_of(f * width, width), width)
    ipart[...] = dot_nt(direction, proj[theirs_h, :]).astype(BF16)
    send(ipart, ipart_in, ip_s.at[0], ip_r.at[0], near_a)
    igrad_ref[...] = dot_nt(direction, proj[mine_h, :])

    for e in range(2):

        @pl.when(has_down)
        def _():
            arrived(block(tleft, e, zz), tb_left.at[zz, e])
            tacc[e, own_t] = tacc[e, own_t] + tleft[e, own_t].astype(F32)

        @pl.when(has_up)
        def _():
            arrived(block(tright, e, zz), tb_right.at[zz, e])
            tacc[e, own_t] = tacc[e, own_t] + tright[e, own_t].astype(F32)

    tnorm = tnorms[own_t][:, 0:1]
    u0 = tbuf[0, own_t].astype(F32) / tnorm
    u1 = tbuf[1, own_t].astype(F32) / tnorm
    b0 = tacc[0, own_t]
    b1 = tacc[1, own_t]
    tdot = jnp.sum(u0 * b0 + u1 * b1, axis=1, keepdims=True)
    factor = scale / tnorm
    tacc[0, own_t] = (b0 - u0 * tdot) * factor
    tacc[1, own_t] = (b1 - u1 * tdot) * factor
    tpart[...] = tacc[1 - f, own_t].astype(BF16)
    send(tpart, tpart_in, tp_s.at[0], tp_r.at[0], near_a)
    tgrad_ref[mine, :] = tacc[f, own_t]

    arrived(ipart_in, ip_r.at[0])
    igrad_ref[...] = igrad_ref[...] + ipart_in[...].astype(F32)
    arrived(tpart_in, tp_r.at[0])
    tgrad_ref[theirs, :] = tpart_in[...].astype(F32)

    for copy in sent:
        copy.wait_send()
    for dist in range(LINE):
        for e in range(2):
            t_forward_sent(dist, e)
        if dist > 0:
            t_back_sent(dist)


def local(image_feats, text_emb, image_proj, log_temp, bias):
    rows, wide = image_feats.shape
    width = text_emb.shape[1]
    dma = pltpu.SemaphoreType.DMA
    group = 4 * rows
    text_rows = LINE * HALF
    return pl.pallas_call(
        kernel,
        out_shape=(jax.ShapeDtypeStruct((rows, width), F32), jax.ShapeDtypeStruct((rows, width), F32)),
        in_specs=[pl.BlockSpec(memory_space=pltpu.HBM)] * 3 + [pl.BlockSpec(memory_space=pltpu.SMEM)] * 2,
        out_specs=(pl.BlockSpec(memory_space=pltpu.VMEM), pl.BlockSpec(memory_space=pltpu.VMEM)),
        scratch_shapes=[
            pltpu.VMEM((rows, wide), BF16),
            pltpu.VMEM((rows, width), BF16),
            pltpu.VMEM((wide, width), BF16),
            pltpu.VMEM((rows, width), F32),
            pltpu.VMEM((2, group, width), BF16),
            pltpu.VMEM((2, text_rows, width), BF16),
            pltpu.VMEM((2, text_rows, width), BF16),
            pltpu.VMEM((text_rows, 128), F32),
            pltpu.VMEM((2, text_rows, width), F32),
            pltpu.VMEM((2, text_rows, width), BF16),
            pltpu.VMEM((2, text_rows, width), BF16),
            pltpu.VMEM((2, text_rows, width), BF16),
            pltpu.VMEM((2, 2 * rows, width), F32),
            pltpu.VMEM((4, rows, width), BF16),
            pltpu.VMEM((4, rows, width), BF16),
            pltpu.VMEM((6, HALF, width), BF16),
            pltpu.VMEM((6, HALF, width), BF16),
            pltpu.VMEM((8, rows), F32),
            pltpu.VMEM((8, rows), F32),
            pltpu.VMEM((group, text_rows), BF16),
            pltpu.VMEM((8, group), F32),
            pltpu.VMEM((3, 8, 2 * rows), F32),
            pltpu.VMEM((3, 8, rows), F32),
            pltpu.VMEM((3, 8, rows), F32),
            pltpu.VMEM((rows, width), BF16),
            pltpu.VMEM((rows, width), BF16),
            pltpu.VMEM((HALF, width), BF16),
            pltpu.VMEM((HALF, width), BF16),
            dma((3,)),
            dma((1,)), dma((1,)),
            dma((6,)), dma((6,)),
            dma((4,)), dma((4,)),
            dma((1,)), dma((4, 2)), dma((4, 2)), dma((4, 2)),
            dma((4, 2)), dma((4, 2)), dma((4, 2)),
            dma((4,)), dma((4,)),
            dma((6,)), dma((6,)),
            dma((1,)), dma((1,)),
            dma((3,)), dma((3,)),
            dma((1,)), dma((1,)),
            dma((1,)), dma((1,)),
        ],
        compiler_params=pltpu.CompilerParams(
            collective_id=0, has_side_effects=True, vmem_limit_bytes=60 << 20
        ),
        name="contrastive_backward",
    )(image_feats, text_emb, image_proj, log_temp, bias)


def solution(mesh):
    placed = (P("dp", None), P("dp", "feat"), P(None, "feat"), P(), P())
    return jax.shard_map(
        local,
        mesh=mesh,
        in_specs=placed,
        out_specs=(P("dp", "feat"), P("dp", "feat")),
        check_vma=False,
    )
```

time: 60.3 us -> 51.4 us (0.85)
  the two profiles are of different devices: /device:TPU:32 before, /device:TPU:8 now
where the time goes in v2:
time: 51.4 us; the launch traced here: 51.1 us
  Pallas kernels  45.7 us (89%)
  local copies, waits for them, and re-layouts  3.53 us (7%)
  between operations  1.93 us (4%)
    pallas_call x1, Pallas kernels, local(): pl.pallas_call(kernel, out_shape=(jax.ShapeDtypeStruct((rows, width), F32...  45.7 us
    unnamed x2, local copies, waits for them, and re-layouts  3.53 us

profile of v2, /device:TPU:8, one launch (start us, length us, event | category | flops | bytes accessed | tf_op | source)
XLA Modules:
  0.0 51.1 jit_solution(7708520593367798998)
XLA Ops:
  1.9 45.7 %contrastive_backward.1 = (f32[128,768]{1,0:T(8,128)}, f32[128,768]{1,0:T(8,128)}) custom-call(bf16[128,1536]{1,0:T(8,128)(2,1)} %feats_hbm.1, bf16[128,768]{1,0:T(8,128)(2,1)} %text_hbm.1, bf16[1536,768]{1,0:T(8,128)(2,1)} %proj_hbm.1, f32[1]{0:T(128)S(6)} %copy.9.temp_ref, f32[1]{0:T(128)S(6)} %copy.10.bias_ref), custom_call_target="tpu_custom_call" | custom-call | tf_op jit(solution)/shard_map/contrastive_backward/pallas_call | solution.py:381
  47.6 1.8 %copy.11 = f32[128,768]{1,0:T(8,128)} copy(f32[128,768]{1,0:T(8,128)} %get-tuple-element.4) | data formatting | bytes 786432
  49.3 1.8 %copy.12 = f32[128,768]{1,0:T(8,128)} copy(f32[128,768]{1,0:T(8,128)} %get-tuple-element.5) | data formatting | bytes 786432

commit v3 on v2

--- a/solution.py
+++ b/solution.py
@@ -14,6 +14,7 @@
 ROWS = 128
 HALF = 64
 LINE = 4
+CUTS = 4
 
 
 def dot_nt(left, right):
@@ -36,10 +37,10 @@
 
 def kernel(
     feats_hbm, text_hbm, proj_hbm, temp_ref, bias_ref, igrad_ref, tgrad_ref,
-    feats, text, proj, iunit32, ibuf, tbuf, tunit, tnorms, tacc, tsend, tleft, tright, qacc, qsend, qrecv,
-    rsend, rrecv, sq_out, sq_in, dots, dot_all, dot_core, dot_out, dot_in, ipart, ipart_in, tpart, tpart_in,
-    lsem, sq_s, sq_r, ig_s, ig_r, core_s, core_r, tf_swap, tf_up, tf_down, tf_r,
-    tb_s, tb_left, tb_right, q_s, q_r, rs_s, rs_r, dc_s, dc_r, dot_s, dot_r, ip_s, ip_r, tp_s, tp_r,
+    feats, text, proj, emb_ref, ibuf, inorms, tbuf, tunit, tnorms, weigh, wimg, tacc, tsend, tleft, tright,
+    qown, qa, qb, rsend, rrecv, dot_out, dot_in, ipart, ipart_in, tpart, tpart_in,
+    lsem, ig_s, ig_r, core_s, core_r, tf_swap, tf_up, tf_down, tf_r, ts_s, ts_r,
+    tb_s, tb_left, tb_right, rs_s, rs_r, dot_s, dot_r, ip_s, ip_r, tp_s, tp_r,
 ):
     dp = lax.axis_index("dp")
     f = lax.axis_index("feat")
@@ -69,13 +70,13 @@
         sent.append(copy)
 
     def arrived(dst, r):
-        remote(dst, dst, q_s.at[0], r, core).wait_recv()
-
-    loads = [
-        pltpu.make_async_copy(text_hbm, text, lsem.at[0]),
-        pltpu.make_async_copy(feats_hbm, feats, lsem.at[1]),
-        pltpu.make_async_copy(proj_hbm, proj, lsem.at[2]),
-    ]
+        remote(dst, dst, tf_swap.at[0], r, core).wait_recv()
+
+    depth = proj.shape[0] // CUTS
+    loads = [pltpu.make_async_copy(text_hbm, text, lsem.at[0]), pltpu.make_async_copy(feats_hbm, feats, lsem.at[1])]
+    for cut in range(CUTS):
+        rows = pl.ds(cut * depth, depth)
+        loads.append(pltpu.make_async_copy(proj_hbm.at[rows], proj.at[rows], lsem.at[2 + cut]))
     for load in loads:
         load.start()
 
@@ -132,6 +133,9 @@
             @pl.when(jnp.logical_and(here, can))
             def _():
                 remote(block(tbuf, e, b), block(tbuf, e, b), sems.at[dist, e], tf_r.at[b, e], to).wait_send()
+
+    def units(core_at, b):
+        return tunit.at[:, pl.ds(pl.multiple_of((core_at * LINE + b) * HALF, HALF), HALF)]
 
     def normalise(b):
         at = rows_of(b)
@@ -139,8 +143,10 @@
         t1 = tbuf[1, at].astype(F32)
         norm = jnp.sqrt(jnp.sum(t0 * t0 + t1 * t1, axis=1, keepdims=True) + EPS)
         tnorms[at] = jnp.broadcast_to(norm, (HALF, 128))
-        tunit[0, at] = (t0 / norm).astype(BF16)
-        tunit[1, at] = (t1 / norm).astype(BF16)
+        to = pl.ds(pl.multiple_of((c * LINE + b) * HALF, HALF), HALF)
+        tunit[0, to] = (t0 / norm).astype(BF16)
+        tunit[1, to] = (t1 / norm).astype(BF16)
+        remote(units(c, b), units(c, b), ts_s.at[b], ts_r.at[b], core).start()
 
     def normalise_at(dist):
         for b, here in ((zz - dist, zz - dist >= 0), (zz + dist, zz + dist < LINE)):
@@ -153,27 +159,27 @@
     tbuf[f, own_t] = text[mine, :]
 
     loads[1].wait()
-    loads[2].wait()
-    emb = dot_nn(feats[...], proj[...])
-    iunit32[...] = emb
-    sq_out[...] = as_row(jnp.sum(emb * emb, axis=1, keepdims=True))
-    send(sq_out, sq_in, sq_s.at[0], sq_r.at[0], near_a)
-
-    arrived(block(tbuf, 1 - f, zz), tf_r.at[zz, 1 - f])
-    t_forward(0, 1 - f)
-    normalise(zz)
-
-    arrived(sq_in, sq_r.at[0])
-    inorm = jnp.sqrt(as_column(sq_out[0:1, :] + sq_in[0:1, :]) + EPS)
-    unit32 = iunit32[...] / inorm
-    iunit32[...] = unit32
+    emb = None
+    for cut in range(CUTS):
+        loads[2 + cut].wait()
+        at = pl.ds(cut * depth, depth)
+        term = dot_nn(feats[:, at], proj[at, :])
+        emb = term if emb is None else emb + term
+    emb_ref[...] = emb
 
     def img(width, core_at, high, part=None):
         start = (core_at * 2 + high) * ROWS + (0 if part is None else part * HALF)
         size = ROWS if part is None else HALF
         return ibuf.at[width, pl.ds(pl.multiple_of(start, HALF), size)]
 
-    ibuf[f, pl.ds(pl.multiple_of((c * 2 + h) * ROWS, ROWS), ROWS)] = unit32.astype(BF16)
+    def inorm_of(core_at, high):
+        at = pl.ds(pl.multiple_of((core_at * 2 + high) * ROWS, ROWS), ROWS)
+        x0 = ibuf[0, at].astype(F32)
+        x1 = ibuf[1, at].astype(F32)
+        norm = jnp.sqrt(jnp.sum(x0 * x0 + x1 * x1, axis=1, keepdims=True) + EPS)
+        inorms[at] = jnp.broadcast_to(norm, (ROWS, 128))
+
+    ibuf[f, pl.ds(pl.multiple_of((c * 2 + h) * ROWS, ROWS), ROWS)] = emb.astype(BF16)
 
     def give(part_ref, slot, to):
         send(part_ref, part_ref, ig_s.at[slot], ig_r.at[slot], to)
@@ -187,15 +193,19 @@
         send(piece, piece, core_s.at[slot], core_r.at[slot], core)
 
     share(img(f, c, h), 0)
+    arrived(block(tbuf, 1 - f, zz), tf_r.at[zz, 1 - f])
+    t_forward(0, 1 - f)
+    normalise(zz)
     t_forward(1, f)
     t_forward(1, 1 - f)
+    normalise_at(1)
     arrived(img(1 - f, c, h, 0), ig_r.at[0])
     give(img(1 - f, c, h, 0), 4, near_b)
     arrived(img(1 - f, c, 1 - h, 1), ig_r.at[3])
     give(img(1 - f, c, 1 - h, 1), 5, near_a)
-    normalise_at(1)
     arrived(img(1 - f, c, h, 1), ig_r.at[1])
     share(img(1 - f, c, h), 1)
+    inorm_of(c, h)
     arrived(img(1 - f, c, 1 - h, 0), ig_r.at[2])
     share(img(1 - f, c, 1 - h), 2)
     t_forward(2, f)
@@ -204,22 +214,31 @@
     arrived(img(f, c, 1 - h, 0), ig_r.at[4])
     arrived(img(f, c, 1 - h, 1), ig_r.at[5])
     share(img(f, c, 1 - h), 3)
+    inorm_of(c, 1 - h)
+    arrived(img(f, 1 - c, h), core_r.at[0])
+    arrived(img(1 - f, 1 - c, h), core_r.at[1])
+    inorm_of(1 - c, h)
+    arrived(img(1 - f, 1 - c, 1 - h), core_r.at[2])
+    arrived(img(f, 1 - c, 1 - h), core_r.at[3])
+    inorm_of(1 - c, 1 - h)
     t_forward(3, f)
     t_forward(3, 1 - f)
     normalise_at(3)
-    arrived(img(f, 1 - c, h), core_r.at[0])
-    arrived(img(1 - f, 1 - c, h), core_r.at[1])
-    arrived(img(1 - f, 1 - c, 1 - h), core_r.at[2])
-    arrived(img(f, 1 - c, 1 - h), core_r.at[3])
-
-    sums = dot_nt(ibuf[0], tunit[0]) + dot_nt(ibuf[1], tunit[1])
-    logits = scale * sums + offset
+
+    text_rows = LINE * HALF
+    t_own = pl.ds(pl.multiple_of(c * text_rows, text_rows), text_rows)
+    t_other = pl.ds(pl.multiple_of((1 - c) * text_rows, text_rows), text_rows)
+    i_own = pl.ds(pl.multiple_of(c * 2 * ROWS, 2 * ROWS), 2 * ROWS)
+    inverse = 1.0 / inorms[...][:, 0:1]
+    cosines = (dot_nt(ibuf[0], tunit[0, t_own]) + dot_nt(ibuf[1], tunit[1, t_own])) * inverse
+    logits = scale * cosines + offset
     row = lax.broadcasted_iota(jnp.int32, logits.shape, 0) - ((c * 2 + h) * ROWS + HALF * f)
     col = lax.broadcasted_iota(jnp.int32, logits.shape, 1) - zz * HALF
     same = jnp.logical_and(row == col, jnp.logical_and(col >= 0, col < HALF))
-    weights32 = jax.nn.sigmoid(logits) - jnp.where(same, 1.0, 0.0)
-    weights = weights32.astype(BF16)
-    weights_t = jnp.transpose(weights32).astype(BF16)
+    weights = jax.nn.sigmoid(logits) - jnp.where(same, 1.0, 0.0)
+    weights_t = jnp.transpose(weights * inverse).astype(BF16)
+    weigh[0] = weights
+    weigh[1] = weights * cosines
 
     for e in range(2):
         tacc[e] = dot_nn(weights_t, ibuf[e])
@@ -261,77 +280,68 @@
 
     t_back(3)
 
-    def quarter(core_at, high, part=None):
-        start = (core_at * 2 + high) * ROWS + (0 if part is None else part * HALF)
+    for b in range(LINE):
+        arrived(units(1 - c, b), ts_r.at[b])
+    inverse = 1.0 / inorms[i_own][:, 0:1]
+    cosines = (dot_nt(ibuf[0, i_own], tunit[0, t_other]) + dot_nt(ibuf[1, i_own], tunit[1, t_other])) * inverse
+    weights = jax.nn.sigmoid(scale * cosines + offset)
+    wimg[:, t_own] = weigh[0, i_own].astype(BF16)
+    wimg[:, t_other] = weights.astype(BF16)
+
+    def mid(high, part=None):
+        start = high * ROWS + (0 if part is None else part * HALF)
         return pl.ds(pl.multiple_of(start, HALF), ROWS if part is None else HALF)
-
-    rows_other = pl.ds(pl.multiple_of((1 - c) * 2 * ROWS, ROWS), 2 * ROWS)
-    rows_own = pl.ds(pl.multiple_of(c * 2 * ROWS, ROWS), 2 * ROWS)
-    wide_weights = dots
-    wide_weights[...] = weights
-    order = ((f, 1 - h), (1 - f, 1 - h), (1 - f, h), (f, h))
-    for slot, (width, high) in enumerate(order):
-        qsend[slot] = dot_nn(wide_weights[quarter(1 - c, high), :], tunit[width]).astype(BF16)
-        send(qsend.at[slot], qrecv.at[slot], q_s.at[slot], q_r.at[slot], core)
-
-    part = jnp.sum(weights32 * sums, axis=1, keepdims=True)
-    dot_all[...] = as_row(part)
-    ds_other = pl.ds(pl.multiple_of((1 - c) * 2 * ROWS, ROWS), 2 * ROWS)
-    ds_own = pl.ds(pl.multiple_of(c * 2 * ROWS, ROWS), 2 * ROWS)
-    dot_core[0] = dot_all[:, ds_other]
-    send(dot_core.at[0], dot_core.at[1], dc_s.at[0], dc_r.at[0], core)
-
-    for e in range(2):
-        qacc[e] = dot_nn(wide_weights[rows_own, :], tunit[e])
-
-    def mid(high, part):
-        return pl.ds(pl.multiple_of(high * ROWS + part * HALF, HALF), HALF)
-
-    def whole(slot, width, high):
-        arrived(qrecv.at[slot], q_r.at[slot])
-        at = pl.ds(pl.multiple_of(high * ROWS, ROWS), ROWS)
-        qacc[width, at] = qacc[width, at] + qrecv[slot].astype(F32)
 
     def hand(slot, value, to):
         rsend[slot] = value.astype(BF16)
         send(rsend.at[slot], rrecv.at[slot], rs_s.at[slot], rs_r.at[slot], to)
 
-    def got(slot):
-        arrived(rrecv.at[slot], rs_r.at[slot])
-        return rrecv[slot].astype(F32)
-
-    whole(0, f, 1 - h)
-    hand(0, qacc[f, mid(1 - h, 0)], near_a)
-    hand(1, qacc[f, mid(1 - h, 1)], near_b)
-    whole(1, 1 - f, 1 - h)
-    hand(5, qacc[1 - f, mid(1 - h, 1)], near_b)
-    whole(2, 1 - f, h)
-    hand(2, qacc[1 - f, mid(h, 0)], near_a)
-    arrived(dot_core.at[1], dc_r.at[0])
-    dot_core[2] = dot_all[:, ds_own] + dot_core[1]
+    value = dot_nn(wimg[mid(1 - h), :], tunit[f])
+    hand(4, value[0:HALF], near_a)
+    hand(5, value[HALF:], near_b)
+    to_b = dot_nn(wimg[mid(1 - h), :], tunit[1 - f])
+    hand(3, to_b[HALF:], near_b)
+    to_a = dot_nn(wimg[mid(h), :], tunit[1 - f])
+    hand(0, to_a[0:HALF], near_a)
+    qa[...] = to_a[HALF:]
+    qb[...] = to_b[0:HALF]
+
+    products = as_row(jnp.sum(weigh[1, i_own] + weights * cosines, axis=1, keepdims=True))
+    dot_out[3, :, 0 : 2 * ROWS] = products
     for slot, high, to in ((0, h, near_a), (1, 1 - h, near_b), (2, 1 - h, far)):
-        dot_out[slot] = dot_core[2, :, pl.ds(pl.multiple_of(high * ROWS, ROWS), ROWS)]
-        send(dot_out.at[slot], dot_in.at[slot], dot_s.at[slot], dot_r.at[slot], to)
-    whole(3, f, h)
+        dot_out[slot, :, 0:ROWS] = dot_out[3, :, pl.ds(pl.multiple_of(high * ROWS, ROWS), ROWS)]
+        at = dot_out.at[slot, :, pl.ds(0, ROWS)]
+        send(at, dot_in.at[slot], dot_s.at[slot], dot_r.at[slot], to)
+    qown[...] = dot_nn(wimg[mid(h), :], tunit[f])
+
     t_back(2)
-    hand(4, qacc[1 - f, mid(1 - h, 0)] + got(0), near_b)
-    hand(3, qacc[1 - f, mid(h, 1)] + got(1), near_a)
+    arrived(rrecv.at[4], rs_r.at[4])
+    hand(2, qb[...] + rrecv[4].astype(F32), near_b)
+    arrived(rrecv.at[5], rs_r.at[5])
+    hand(1, qa[...] + rrecv[5].astype(F32), near_a)
     t_back(1)
 
     for slot in range(3):
         arrived(dot_in.at[slot], dot_r.at[slot])
-    idot_row = dot_core[2, 0:1, pl.ds(pl.multiple_of(h * ROWS, ROWS), ROWS)]
+    idot_row = dot_out[3, 0:1, pl.ds(pl.multiple_of(h * ROWS, ROWS), ROWS)]
     idot = as_column(idot_row + dot_in[0, 0:1, :] + dot_in[1, 0:1, :] + dot_in[2, 0:1, :])
-    low = qacc[f, mid(h, 0)] + got(2) + got(4)
-    high = qacc[f, mid(h, 1)] + got(5) + got(3)
-    back = jnp.concatenate([low, high], axis=0)
-    direction = ((back - iunit32[...] * idot) * (scale / inorm)).astype(BF16)
     width = proj.shape[1]
     theirs_h = pl.ds(pl.multiple_of((1 - f) * width, width), width)
     mine_h = pl.ds(pl.multiple_of(f * width, width), width)
-    ipart[...] = dot_nt(direction, proj[theirs_h, :]).astype(BF16)
-    send(ipart, ipart_in, ip_s.at[0], ip_r.at[0], near_a)
-    igrad_ref[...] = dot_nt(direction, proj[mine_h, :])
+    inorm = inorms[pl.ds(pl.multiple_of((c * 2 + h) * ROWS, ROWS), ROWS)][:, 0:1]
+    directions = []
+    for part in range(2):
+        at = pl.ds(part * HALF, HALF)
+        for slot in (part, 2 + part):
+            arrived(rrecv.at[slot], rs_r.at[slot])
+        back = qown[at] + (rrecv[part].astype(F32) + rrecv[2 + part].astype(F32))
+        norm = inorm[part * HALF : part * HALF + HALF]
+        unit = emb_ref[at] / norm
+        direction = ((back - unit * idot[part * HALF : part * HALF + HALF]) * (scale / norm)).astype(BF16)
+        ipart[at] = dot_nt(direction, proj[theirs_h, :]).astype(BF16)
+        send(ipart.at[at], ipart_in.at[at], ip_s.at[part], ip_r.at[part], near_a)
+        directions.append(direction)
+    igrad_ref[...] = dot_nt(jnp.concatenate(directions, axis=0), proj[mine_h, :])
 
     for e in range(2):
 
@@ -358,13 +368,17 @@
     send(tpart, tpart_in, tp_s.at[0], tp_r.at[0], near_a)
     tgrad_ref[mine, :] = tacc[f, own_t]
 
-    arrived(ipart_in, ip_r.at[0])
-    igrad_ref[...] = igrad_ref[...] + ipart_in[...].astype(F32)
+    for part in range(2):
+        at = pl.ds(part * HALF, HALF)
+        arrived(ipart_in.at[at], ip_r.at[part])
+        igrad_ref[at, :] = igrad_ref[at, :] + ipart_in[at].astype(F32)
     arrived(tpart_in, tp_r.at[0])
     tgrad_ref[theirs, :] = tpart_in[...].astype(F32)
 
     for copy in sent:
         copy.wait_send()
+    for b in range(LINE):
+        remote(units(c, b), units(c, b), ts_s.at[b], ts_r.at[b], core).wait_send()
     for dist in range(LINE):
         for e in range(2):
             t_forward_sent(dist, e)
@@ -380,7 +394,7 @@
     text_rows = LINE * HALF
     return pl.pallas_call(
         kernel,
-        out_shape=(jax.ShapeDtypeStruct((rows, width), F32), jax.ShapeDtypeStruct((rows, width), F32)),
+        out_shape=(pltpu.VMEM((rows, width), F32), pltpu.VMEM((rows, width), F32)),
         in_specs=[pl.BlockSpec(memory_space=pltpu.HBM)] * 3 + [pl.BlockSpec(memory_space=pltpu.SMEM)] * 2,
         out_specs=(pl.BlockSpec(memory_space=pltpu.VMEM), pl.BlockSpec(memory_space=pltpu.VMEM)),
         scratch_shapes=[
@@ -389,47 +403,43 @@
             pltpu.VMEM((wide, width), BF16),
             pltpu.VMEM((rows, width), F32),
             pltpu.VMEM((2, group, width), BF16),
+            pltpu.VMEM((group, 128), F32),
             pltpu.VMEM((2, text_rows, width), BF16),
-            pltpu.VMEM((2, text_rows, width), BF16),
+            pltpu.VMEM((2, 2 * text_rows, width), BF16),
             pltpu.VMEM((text_rows, 128), F32),
+            pltpu.VMEM((2, group, text_rows), F32),
+            pltpu.VMEM((2 * rows, 2 * text_rows), BF16),
             pltpu.VMEM((2, text_rows, width), F32),
             pltpu.VMEM((2, text_rows, width), BF16),
             pltpu.VMEM((2, text_rows, width), BF16),
             pltpu.VMEM((2, text_rows, width), BF16),
-            pltpu.VMEM((2, 2 * rows, width), F32),
-            pltpu.VMEM((4, rows, width), BF16),
-            pltpu.VMEM((4, rows, width), BF16),
+            pltpu.VMEM((rows, width), F32),
+            pltpu.VMEM((HALF, width), F32),
+            pltpu.VMEM((HALF, width), F32),
             pltpu.VMEM((6, HALF, width), BF16),
             pltpu.VMEM((6, HALF, width), BF16),
-            pltpu.VMEM((8, rows), F32),
-            pltpu.VMEM((8, rows), F32),
-            pltpu.VMEM((group, text_rows), BF16),
-            pltpu.VMEM((8, group), F32),
-            pltpu.VMEM((3, 8, 2 * rows), F32),
-            pltpu.VMEM((3, 8, rows), F32),
+            pltpu.VMEM((4, 8, 2 * rows), F32),
             pltpu.VMEM((3, 8, rows), F32),
             pltpu.VMEM((rows, width), BF16),
             pltpu.VMEM((rows, width), BF16),
             pltpu.VMEM((HALF, width), BF16),
             pltpu.VMEM((HALF, width), BF16),
-            dma((3,)),
-            dma((1,)), dma((1,)),
+            dma((2 + CUTS,)),
             dma((6,)), dma((6,)),
             dma((4,)), dma((4,)),
             dma((1,)), dma((4, 2)), dma((4, 2)), dma((4, 2)),
+            dma((4,)), dma((4,)),
             dma((4, 2)), dma((4, 2)), dma((4, 2)),
-            dma((4,)), dma((4,)),
             dma((6,)), dma((6,)),
-            dma((1,)), dma((1,)),
             dma((3,)), dma((3,)),
-            dma((1,)), dma((1,)),
+            dma((2,)), dma((2,)),
             dma((1,)), dma((1,)),
         ],
         compiler_params=pltpu.CompilerParams(
-            collective_id=0, has_side_effects=True, vmem_limit_bytes=60 << 20
+            collective_id=0, has_side_effects=True, vmem_limit_bytes=48 << 20
         ),
         name="contrastive_backward",
-    )(image_feats, text_emb, image_proj, log_temp, bias)
+    )(*[pltpu.with_memory_space_constraint(x, pltpu.HBM) for x in (image_feats, text_emb, image_proj)], log_temp, bias)
 
 
 def solution(mesh):

time: 51.4 us -> 46.4 us (0.903)
  the two profiles are of different devices: /device:TPU:8 before, /device:TPU:32 now
where the time goes in v3:
time: 46.4 us; the launch traced here: 46.2 us
  Pallas kernels  42.8 us (92%)
  between operations  1.93 us (4%)
  local copies, waits for them, and re-layouts  1.49 us (3%)
    pallas_call x1, Pallas kernels, local(): pl.pallas_call(kernel, out_shape=(pltpu.VMEM((rows, width), F32), pltpu.V...  42.8 us
    unnamed x2, local copies, waits for them, and re-layouts  1.49 us

profile of v3, /device:TPU:32, one launch (start us, length us, event | category | flops | bytes accessed | tf_op | source)
XLA Modules:
  0.0 46.2 jit_solution(10258873898027967413)
XLA Ops:
  1.9 42.8 %contrastive_backward.1 = (f32[128,768]{1,0:T(8,128)S(1)}, f32[128,768]{1,0:T(8,128)S(1)}) custom-call(bf16[128,1536]{1,0:T(8,128)(2,1)} %feats_hbm.1, bf16[128,768]{1,0:T(8,128)(2,1)} %text_hbm.1, bf16[1536,768]{1,0:T(8,128)(2,1)} %proj_hbm.1, f32[1]{0:T(128)S(6)} %copy.11.temp_ref, f32[1]{0:T(128)S(6)} %copy.12.bias_ref), custom_call_target="tpu_custom_call" | custom-call | tf_op jit(solution)/shard_map/contrastive_backward/pallas_call | solution.py:395
  44.7 0.7 %copy.9 = f32[128,768]{1,0:T(8,128)} copy(f32[128,768]{1,0:T(8,128)S(1)} %get-tuple-element.2) | data formatting | bytes 786432
  45.5 0.7 %copy.10 = f32[128,768]{1,0:T(8,128)} copy(f32[128,768]{1,0:T(8,128)S(1)} %get-tuple-element.3) | data formatting | bytes 786432

commit v4 on v3

--- a/solution.py
+++ b/solution.py
@@ -15,6 +15,8 @@
 HALF = 64
 LINE = 4
 CUTS = 4
+FORTH = 2
+BACK = 1
 
 
 def dot_nt(left, right):
@@ -68,6 +70,12 @@
         copy = remote(src, dst, s, r, to)
         copy.start()
         sent.append(copy)
+        return copy
+
+    def left(*copies):
+        for copy in copies:
+            copy.wait_send()
+            sent[:] = [other for other in sent if other is not copy]
 
     def arrived(dst, r):
         remote(dst, dst, tf_swap.at[0], r, core).wait_recv()
@@ -104,35 +112,50 @@
     def rows_of(b):
         return pl.ds(pl.multiple_of(b * HALF, HALF), HALF)
 
-    def block(ref, e, b):
-        return ref.at[e, rows_of(b)]
+    def block(ref, e, b, k=0, pieces=1):
+        size = HALF // pieces
+        return ref.at[e, pl.ds(pl.multiple_of(b * HALF + k * size, size), size)]
 
     own_t = rows_of(zz)
-    send(text.at[theirs], block(tbuf, f, zz), tf_swap.at[0], tf_r.at[zz, f], near_a)
-
-    def t_forward(dist, e, src=None):
-        for sign, can, to, sems in ((-1, has_up, z_up, tf_up), (1, has_down, z_down, tf_down)):
-            b = zz + sign * dist
-            here = (b >= 0) if sign < 0 else (b < LINE)
-
-            @pl.when(here)
-            def _():
-                if dist > 0:
-                    arrived(block(tbuf, e, b), tf_r.at[b, e])
-
-                @pl.when(can)
+    for k in range(FORTH):
+        piece = text.at[pl.ds(pl.multiple_of(HALF * (1 - f) + k * (HALF // FORTH), HALF // FORTH), HALF // FORTH)]
+        send(piece, block(tbuf, f, zz, k, FORTH), tf_swap.at[k], tf_r.at[zz, f * FORTH + k], near_a)
+
+    def t_forward(dist, e, src=False):
+        for k in range(FORTH):
+            for sign, can, to, sems in ((-1, has_up, z_up, tf_up), (1, has_down, z_down, tf_down)):
+                b = zz + sign * dist
+                here = (b >= 0) if sign < 0 else (b < LINE)
+                sem = e * FORTH + k
+
+                @pl.when(here)
                 def _():
-                    origin = block(tbuf, e, b) if src is None else src
-                    remote(origin, block(tbuf, e, b), sems.at[dist, e], tf_r.at[b, e], to).start()
+                    piece = block(tbuf, e, b, k, FORTH)
+                    if dist > 0:
+                        arrived(piece, tf_r.at[b, sem])
+                    elif not src:
+                        if sign < 0:
+                            arrived(piece, tf_r.at[b, sem])
+
+                    @pl.when(can)
+                    def _():
+                        origin = piece
+                        if src:
+                            size = HALF // FORTH
+                            origin = text.at[pl.ds(pl.multiple_of(HALF * f + k * size, size), size)]
+                        remote(origin, piece, sems.at[dist, sem], tf_r.at[b, sem], to).start()
 
     def t_forward_sent(dist, e):
-        for sign, can, to, sems in ((-1, has_up, z_up, tf_up), (1, has_down, z_down, tf_down)):
-            b = zz + sign * dist
-            here = (b >= 0) if sign < 0 else (b < LINE)
-
-            @pl.when(jnp.logical_and(here, can))
-            def _():
-                remote(block(tbuf, e, b), block(tbuf, e, b), sems.at[dist, e], tf_r.at[b, e], to).wait_send()
+        for k in range(FORTH):
+            for sign, can, to, sems in ((-1, has_up, z_up, tf_up), (1, has_down, z_down, tf_down)):
+                b = zz + sign * dist
+                here = (b >= 0) if sign < 0 else (b < LINE)
+                sem = e * FORTH + k
+
+                @pl.when(jnp.logical_and(here, can))
+                def _():
+                    piece = block(tbuf, e, b, k, FORTH)
+                    remote(piece, piece, sems.at[dist, sem], tf_r.at[b, sem], to).wait_send()
 
     def units(core_at, b):
         return tunit.at[:, pl.ds(pl.multiple_of((core_at * LINE + b) * HALF, HALF), HALF)]
@@ -155,7 +178,7 @@
             def _():
                 normalise(b)
 
-    t_forward(0, f, text.at[mine])
+    t_forward(0, f, True)
     tbuf[f, own_t] = text[mine, :]
 
     loads[1].wait()
@@ -182,7 +205,7 @@
     ibuf[f, pl.ds(pl.multiple_of((c * 2 + h) * ROWS, ROWS), ROWS)] = emb.astype(BF16)
 
     def give(part_ref, slot, to):
-        send(part_ref, part_ref, ig_s.at[slot], ig_r.at[slot], to)
+        return send(part_ref, part_ref, ig_s.at[slot], ig_r.at[slot], to)
 
     give(img(f, c, h, 0), 0, near_a)
     give(img(f, c, h, 1), 3, near_b)
@@ -193,7 +216,6 @@
         send(piece, piece, core_s.at[slot], core_r.at[slot], core)
 
     share(img(f, c, h), 0)
-    arrived(block(tbuf, 1 - f, zz), tf_r.at[zz, 1 - f])
     t_forward(0, 1 - f)
     normalise(zz)
     t_forward(1, f)
@@ -245,27 +267,30 @@
 
     def t_back(dist):
         for e in range(2):
-            for sign, can, to, inbox, r in (
-                (-1, has_up, z_down, tright, tb_right),
-                (1, has_down, z_up, tleft, tb_left),
-            ):
-                b = zz + sign * dist
-                here = (b >= 0) if sign < 0 else (b < LINE)
-
-                @pl.when(here)
-                def _():
-                    at = rows_of(b)
-
-                    @pl.when(can)
+            for k in range(BACK):
+                for sign, can, to, inbox, r in (
+                    (-1, has_up, z_down, tright, tb_right),
+                    (1, has_down, z_up, tleft, tb_left),
+                ):
+                    b = zz + sign * dist
+                    here = (b >= 0) if sign < 0 else (b < LINE)
+                    size = HALF // BACK
+                    sem = e * BACK + k
+
+                    @pl.when(here)
                     def _():
-                        arrived(inbox.at[e, at], r.at[b, e])
-                        tsend[e, at] = (tacc[e, at] + inbox[e, at].astype(F32)).astype(BF16)
-
-                    @pl.when(jnp.logical_not(can))
-                    def _():
-                        tsend[e, at] = tacc[e, at].astype(BF16)
-
-                    remote(tsend.at[e, at], inbox.at[e, at], tb_s.at[b, e], r.at[b, e], to).start()
+                        at = pl.ds(pl.multiple_of(b * HALF + k * size, size), size)
+
+                        @pl.when(can)
+                        def _():
+                            arrived(inbox.at[e, at], r.at[b, sem])
+                            tsend[e, at] = (tacc[e, at] + inbox[e, at].astype(F32)).astype(BF16)
+
+                        @pl.when(jnp.logical_not(can))
+                        def _():
+                            tsend[e, at] = tacc[e, at].astype(BF16)
+
+                        remote(tsend.at[e, at], inbox.at[e, at], tb_s.at[b, sem], r.at[b, sem], to).start()
 
     def t_back_sent(dist):
         for sign, to, inbox, r in ((-1, z_down, tright, tb_right), (1, z_up, tleft, tb_left)):
@@ -274,9 +299,12 @@
 
             @pl.when(here)
             def _():
-                at = rows_of(b)
                 for e in range(2):
-                    remote(tsend.at[e, at], inbox.at[e, at], tb_s.at[b, e], r.at[b, e], to).wait_send()
+                    for k in range(BACK):
+                        at = block(tsend, e, b, k, BACK)
+                        into = block(inbox, e, b, k, BACK)
+                        sem = e * BACK + k
+                        remote(at, into, tb_s.at[b, sem], r.at[b, sem], to).wait_send()
 
     t_back(3)
 
@@ -294,17 +322,15 @@
 
     def hand(slot, value, to):
         rsend[slot] = value.astype(BF16)
-        send(rsend.at[slot], rrecv.at[slot], rs_s.at[slot], rs_r.at[slot], to)
+        return send(rsend.at[slot], rrecv.at[slot], rs_s.at[slot], rs_r.at[slot], to)
 
     value = dot_nn(wimg[mid(1 - h), :], tunit[f])
-    hand(4, value[0:HALF], near_a)
-    hand(5, value[HALF:], near_b)
+    first = (hand(4, value[0:HALF], near_a), hand(5, value[HALF:], near_b))
     to_b = dot_nn(wimg[mid(1 - h), :], tunit[1 - f])
-    hand(3, to_b[HALF:], near_b)
     to_a = dot_nn(wimg[mid(h), :], tunit[1 - f])
-    hand(0, to_a[0:HALF], near_a)
     qa[...] = to_a[HALF:]
     qb[...] = to_b[0:HALF]
+    qown[...] = dot_nn(wimg[mid(h), :], tunit[f])
 
     products = as_row(jnp.sum(weigh[1, i_own] + weights * cosines, axis=1, keepdims=True))
     dot_out[3, :, 0 : 2 * ROWS] = products
@@ -312,7 +338,9 @@
         dot_out[slot, :, 0:ROWS] = dot_out[3, :, pl.ds(pl.multiple_of(high * ROWS, ROWS), ROWS)]
         at = dot_out.at[slot, :, pl.ds(0, ROWS)]
         send(at, dot_in.at[slot], dot_s.at[slot], dot_r.at[slot], to)
-    qown[...] = dot_nn(wimg[mid(h), :], tunit[f])
+    left(*first)
+    hand(3, to_b[HALF:], near_b)
+    hand(0, to_a[0:HALF], near_a)
 
     t_back(2)
     arrived(rrecv.at[4], rs_r.at[4])
@@ -347,12 +375,14 @@
 
         @pl.when(has_down)
         def _():
-            arrived(block(tleft, e, zz), tb_left.at[zz, e])
+            for k in range(BACK):
+                arrived(block(tleft, e, zz, k, BACK), tb_left.at[zz, e * BACK + k])
             tacc[e, own_t] = tacc[e, own_t] + tleft[e, own_t].astype(F32)
 
         @pl.when(has_up)
         def _():
-            arrived(block(tright, e, zz), tb_right.at[zz, e])
+            for k in range(BACK):
+                arrived(block(tright, e, zz, k, BACK), tb_right.at[zz, e * BACK + k])
             tacc[e, own_t] = tacc[e, own_t] + tright[e, own_t].astype(F32)
 
     tnorm = tnorms[own_t][:, 0:1]
@@ -386,13 +416,24 @@
             t_back_sent(dist)
 
 
+def store(igrad_vmem, tgrad_vmem, igrad_ref, tgrad_ref, sems):
+    copies = [
+        pltpu.make_async_copy(igrad_vmem, igrad_ref, sems.at[0]),
+        pltpu.make_async_copy(tgrad_vmem, tgrad_ref, sems.at[1]),
+    ]
+    for copy in copies:
+        copy.start()
+    for copy in copies:
+        copy.wait()
+
+
 def local(image_feats, text_emb, image_proj, log_temp, bias):
     rows, wide = image_feats.shape
     width = text_emb.shape[1]
     dma = pltpu.SemaphoreType.DMA
     group = 4 * rows
     text_rows = LINE * HALF
-    return pl.pallas_call(
+    igrad, tgrad = pl.pallas_call(
         kernel,
         out_shape=(pltpu.VMEM((rows, width), F32), pltpu.VMEM((rows, width), F32)),
         in_specs=[pl.BlockSpec(memory_space=pltpu.HBM)] * 3 + [pl.BlockSpec(memory_space=pltpu.SMEM)] * 2,
@@ -427,9 +468,9 @@
             dma((2 + CUTS,)),
             dma((6,)), dma((6,)),
             dma((4,)), dma((4,)),
-            dma((1,)), dma((4, 2)), dma((4, 2)), dma((4, 2)),
+            dma((FORTH,)), dma((4, 2 * FORTH)), dma((4, 2 * FORTH)), dma((4, 2 * FORTH)),
             dma((4,)), dma((4,)),
-            dma((4, 2)), dma((4, 2)), dma((4, 2)),
+            dma((4, 2 * BACK)), dma((4, 2 * BACK)), dma((4, 2 * BACK)),
             dma((6,)), dma((6,)),
             dma((3,)), dma((3,)),
             dma((2,)), dma((2,)),
@@ -440,6 +481,16 @@
         ),
         name="contrastive_backward",
     )(*[pltpu.with_memory_space_constraint(x, pltpu.HBM) for x in (image_feats, text_emb, image_proj)], log_temp, bias)
+    shape = jax.ShapeDtypeStruct((rows, width), F32)
+    return pl.pallas_call(
+        store,
+        out_shape=(shape, shape),
+        in_specs=[pl.BlockSpec(memory_space=pl.ANY)] * 2,
+        out_specs=(pl.BlockSpec(memory_space=pl.ANY), pl.BlockSpec(memory_space=pl.ANY)),
+        scratch_shapes=[dma((2,))],
+        compiler_params=pltpu.CompilerParams(vmem_limit_bytes=1 << 20),
+        name="store_gradients",
+    )(*[pltpu.with_memory_space_constraint(x, pltpu.VMEM) for x in (igrad, tgrad)])
 
 
 def solution(mesh):

time: 46.4 us -> 45.1 us (0.972)
  local copies, waits for them, and re-layouts: 1.49 us -> 0 us
    unnamed x2 -> x0, local copies, waits for them, and re-layouts: 1.49 us -> none
    pallas_call x0 -> x1, Pallas kernels: none -> 0.89 us  [local(): pl.pallas_call(store, out_shape=(shape, shape), in_specs=[pl.BlockSpec(me...]
    pallas_call x1, Pallas kernels: 42.8 us -> 42.1 us  [local(): pl.pallas_call(kernel, out_shape=(pltpu.VMEM((rows, width), F32), pltpu.V...]
where the time goes in v4:
time: 45.1 us; the launch traced here: 44.9 us
  Pallas kernels  43 us (95%)
  between operations  1.93 us (4%)
    pallas_call x1, Pallas kernels, local(): pl.pallas_call(kernel, out_shape=(pltpu.VMEM((rows, width), F32), pltpu.V...  42.1 us

profile of v4, /device:TPU:32, one launch (start us, length us, event | category | flops | bytes accessed | tf_op | source)
XLA Modules:
  0.0 44.9 jit_solution(478164884948380004)
XLA Ops:
  1.9 42.1 %contrastive_backward.1 = (f32[128,768]{1,0:T(8,128)S(1)}, f32[128,768]{1,0:T(8,128)S(1)}) custom-call(bf16[128,1536]{1,0:T(8,128)(2,1)} %feats_hbm.1, bf16[128,768]{1,0:T(8,128)(2,1)} %text_hbm.1, bf16[1536,768]{1,0:T(8,128)(2,1)} %proj_hbm.1, f32[1]{0:T(128)S(6)} %copy.7.temp_ref, f32[1]{0:T(128)S(6)} %copy.8.bias_ref), custom_call_target="tpu_custom_call" | custom-call | tf_op jit(solution)/shard_map/contrastive_backward/pallas_call | solution.py:436
  44.0 0.9 %store_gradients.1 = (f32[128,768]{1,0:T(8,128)}, f32[128,768]{1,0:T(8,128)}) custom-call(f32[128,768]{1,0:T(8,128)S(1)} %get-tuple-element.4.igrad_vmem, f32[128,768]{1,0:T(8,128)S(1)} %get-tuple-element.5.tgrad_vmem), custom_call_target="tpu_custom_call" | custom-call | tf_op jit(solution)/shard_map/store_gradients/pallas_call | solution.py:485

commit v5 on v4

--- a/solution.py
+++ b/solution.py
@@ -14,7 +14,7 @@
 ROWS = 128
 HALF = 64
 LINE = 4
-CUTS = 4
+CUTS = 2
 FORTH = 2
 BACK = 1
 
@@ -262,11 +262,9 @@
     weigh[0] = weights
     weigh[1] = weights * cosines
 
-    for e in range(2):
-        tacc[e] = dot_nn(weights_t, ibuf[e])
-
-    def t_back(dist):
-        for e in range(2):
+
+    def t_back(dist, halves=(0, 1)):
+        for e in halves:
             for k in range(BACK):
                 for sign, can, to, inbox, r in (
                     (-1, has_up, z_down, tright, tb_right),
@@ -306,7 +304,8 @@
                         sem = e * BACK + k
                         remote(at, into, tb_s.at[b, sem], r.at[b, sem], to).wait_send()
 
-    t_back(3)
+    tacc[0] = dot_nn(weights_t, ibuf[0])
+    t_back(3, (0,))
 
     for b in range(LINE):
         arrived(units(1 - c, b), ts_r.at[b])
@@ -326,6 +325,8 @@
 
     value = dot_nn(wimg[mid(1 - h), :], tunit[f])
     first = (hand(4, value[0:HALF], near_a), hand(5, value[HALF:], near_b))
+    tacc[1] = dot_nn(weights_t, ibuf[1])
+    t_back(3, (1,))
     to_b = dot_nn(wimg[mid(1 - h), :], tunit[1 - f])
     to_a = dot_nn(wimg[mid(h), :], tunit[1 - f])
     qa[...] = to_a[HALF:]
@@ -369,7 +370,6 @@
         ipart[at] = dot_nt(direction, proj[theirs_h, :]).astype(BF16)
         send(ipart.at[at], ipart_in.at[at], ip_s.at[part], ip_r.at[part], near_a)
         directions.append(direction)
-    igrad_ref[...] = dot_nt(jnp.concatenate(directions, axis=0), proj[mine_h, :])
 
     for e in range(2):
 
@@ -385,24 +385,30 @@
                 arrived(block(tright, e, zz, k, BACK), tb_right.at[zz, e * BACK + k])
             tacc[e, own_t] = tacc[e, own_t] + tright[e, own_t].astype(F32)
 
-    tnorm = tnorms[own_t][:, 0:1]
-    u0 = tbuf[0, own_t].astype(F32) / tnorm
-    u1 = tbuf[1, own_t].astype(F32) / tnorm
-    b0 = tacc[0, own_t]
-    b1 = tacc[1, own_t]
-    tdot = jnp.sum(u0 * b0 + u1 * b1, axis=1, keepdims=True)
-    factor = scale / tnorm
-    tacc[0, own_t] = (b0 - u0 * tdot) * factor
-    tacc[1, own_t] = (b1 - u1 * tdot) * factor
-    tpart[...] = tacc[1 - f, own_t].astype(BF16)
-    send(tpart, tpart_in, tp_s.at[0], tp_r.at[0], near_a)
+    for part in range(2):
+        size = HALF // 2
+        at = pl.ds(pl.multiple_of(zz * HALF + part * size, size), size)
+        norm = tnorms[at][:, 0:1]
+        u0 = tbuf[0, at].astype(F32) / norm
+        u1 = tbuf[1, at].astype(F32) / norm
+        b0 = tacc[0, at]
+        b1 = tacc[1, at]
+        tdot = jnp.sum(u0 * b0 + u1 * b1, axis=1, keepdims=True)
+        factor = scale / norm
+        tacc[0, at] = (b0 - u0 * tdot) * factor
+        tacc[1, at] = (b1 - u1 * tdot) * factor
+        to = pl.ds(part * size, size)
+        tpart[to] = tacc[1 - f, at].astype(BF16)
+        send(tpart.at[to], tpart_in.at[to], tp_s.at[part], tp_r.at[part], near_a)
     tgrad_ref[mine, :] = tacc[f, own_t]
+    igrad_ref[...] = dot_nt(jnp.concatenate(directions, axis=0), proj[mine_h, :])
 
     for part in range(2):
         at = pl.ds(part * HALF, HALF)
         arrived(ipart_in.at[at], ip_r.at[part])
         igrad_ref[at, :] = igrad_ref[at, :] + ipart_in[at].astype(F32)
-    arrived(tpart_in, tp_r.at[0])
+    for part in range(2):
+        arrived(tpart_in.at[pl.ds(part * (HALF // 2), HALF // 2)], tp_r.at[part])
     tgrad_ref[theirs, :] = tpart_in[...].astype(F32)
 
     for copy in sent:
@@ -474,7 +480,7 @@
             dma((6,)), dma((6,)),
             dma((3,)), dma((3,)),
             dma((2,)), dma((2,)),
-            dma((1,)), dma((1,)),
+            dma((2,)), dma((2,)),
         ],
         compiler_params=pltpu.CompilerParams(
             collective_id=0, has_side_effects=True, vmem_limit_bytes=48 << 20

time: 45.1 us -> 44.5 us (0.987)
  Pallas kernels: 43 us -> 42.4 us
    pallas_call x1, Pallas kernels: 42.1 us -> 41.5 us  [local(): pl.pallas_call(kernel, out_shape=(pltpu.VMEM((rows, width), F32), pltpu.V...]
where the time goes in v5:
time: 44.5 us; the launch traced here: 44.4 us
  Pallas kernels  42.4 us (95%)
  between operations  1.93 us (4%)
    pallas_call x1, Pallas kernels, local(): pl.pallas_call(kernel, out_shape=(pltpu.VMEM((rows, width), F32), pltpu.V...  41.5 us
    pallas_call x1, Pallas kernels, local(): pl.pallas_call(store, out_shape=(shape, shape), in_specs=[pl.BlockSpec(me...  0.89 us

profile of v5, /device:TPU:32, one launch (start us, length us, event | category | flops | bytes accessed | tf_op | source)
XLA Modules:
  0.0 44.4 jit_solution(6242733451748658739)
XLA Ops:
  1.9 41.5 %contrastive_backward.1 = (f32[128,768]{1,0:T(8,128)S(1)}, f32[128,768]{1,0:T(8,128)S(1)}) custom-call(bf16[128,1536]{1,0:T(8,128)(2,1)} %feats_hbm.1, bf16[128,768]{1,0:T(8,128)(2,1)} %text_hbm.1, bf16[1536,768]{1,0:T(8,128)(2,1)} %proj_hbm.1, f32[1]{0:T(128)S(6)} %copy.7.temp_ref, f32[1]{0:T(128)S(6)} %copy.8.bias_ref), custom_call_target="tpu_custom_call" | custom-call | tf_op jit(solution)/shard_map/contrastive_backward/pallas_call | solution.py:442
  43.5 0.9 %store_gradients.1 = (f32[128,768]{1,0:T(8,128)}, f32[128,768]{1,0:T(8,128)}) custom-call(f32[128,768]{1,0:T(8,128)S(1)} %get-tuple-element.4.igrad_vmem, f32[128,768]{1,0:T(8,128)S(1)} %get-tuple-element.5.tgrad_vmem), custom_call_target="tpu_custom_call" | custom-call | tf_op jit(solution)/shard_map/store_gradients/pallas_call | solution.py:491

commit v6 on v5

--- a/solution.py
+++ b/solution.py
@@ -13,6 +13,7 @@
 BF16 = jnp.bfloat16
 ROWS = 128
 HALF = 64
+LONG = 96
 LINE = 4
 CUTS = 2
 FORTH = 2
@@ -191,9 +192,9 @@
     emb_ref[...] = emb
 
     def img(width, core_at, high, part=None):
-        start = (core_at * 2 + high) * ROWS + (0 if part is None else part * HALF)
-        size = ROWS if part is None else HALF
-        return ibuf.at[width, pl.ds(pl.multiple_of(start, HALF), size)]
+        start = (core_at * 2 + high) * ROWS + (0 if part is None else part * LONG)
+        size = ROWS if part is None else (LONG, ROWS - LONG)[part]
+        return ibuf.at[width, pl.ds(pl.multiple_of(start, ROWS - LONG), size)]
 
     def inorm_of(core_at, high):
         at = pl.ds(pl.multiple_of((core_at * 2 + high) * ROWS, ROWS), ROWS)

time: 44.5 us -> 44.5 us (level)
  no operation moved by 1% of the time
where the time goes in v6:
time: 44.5 us; the launch traced here: 44.4 us
  Pallas kernels  42.4 us (95%)
  between operations  1.93 us (4%)
    pallas_call x1, Pallas kernels, local(): pl.pallas_call(kernel, out_shape=(pltpu.VMEM((rows, width), F32), pltpu.V...  41.5 us
    pallas_call x1, Pallas kernels, local(): pl.pallas_call(store, out_shape=(shape, shape), in_specs=[pl.BlockSpec(me...  0.89 us

profile of v6, /device:TPU:32, one launch (start us, length us, event | category | flops | bytes accessed | tf_op | source)
XLA Modules:
  0.0 44.4 jit_solution(4101616171500949493)
XLA Ops:
  1.9 41.5 %contrastive_backward.1 = (f32[128,768]{1,0:T(8,128)S(1)}, f32[128,768]{1,0:T(8,128)S(1)}) custom-call(bf16[128,1536]{1,0:T(8,128)(2,1)} %feats_hbm.1, bf16[128,768]{1,0:T(8,128)(2,1)} %text_hbm.1, bf16[1536,768]{1,0:T(8,128)(2,1)} %proj_hbm.1, f32[1]{0:T(128)S(6)} %copy.7.temp_ref, f32[1]{0:T(128)S(6)} %copy.8.bias_ref), custom_call_target="tpu_custom_call" | custom-call | tf_op jit(solution)/shard_map/contrastive_backward/pallas_call | solution.py:443
  43.5 0.9 %store_gradients.1 = (f32[128,768]{1,0:T(8,128)}, f32[128,768]{1,0:T(8,128)}) custom-call(f32[128,768]{1,0:T(8,128)S(1)} %get-tuple-element.4.igrad_vmem, f32[128,768]{1,0:T(8,128)S(1)} %get-tuple-element.5.tgrad_vmem), custom_call_target="tpu_custom_call" | custom-call | tf_op jit(solution)/shard_map/store_gradients/pallas_call | solution.py:492
